TPU v7x, 32 devices: a whole 2x2x4 slice. The times are simulated.
32 devices in a mesh: rows: 4 (over y, x), vocab: 8 (over z, core).
Axes of the slice: x: 2, y: 2, z: 4, core: 2. Of those that a mesh axis runs over, the one named last changes fastest.
Arguments:
- tokens: int32 [4096], P('rows'), may hold values from 0 to 50303
- loss_position_mask: int32 [4096], P('rows'), may hold values from 0 to 1
- lengths: int32 [4, 5], P('rows'), may hold values from 1 to 512, 1024 in all within a row
- owners: int32 [32], replicated, may hold values from 0 to 31, each once
- embed_in: bfloat16 [50304, 1024], P('vocab'), may hold values from -6 to 6
- unembedding_table: bfloat16 [50304, 1024], P('vocab'), may hold values from -0.375 to 0.375
- frozen_qkv: bfloat16 [1024, 3072], replicated, may hold values from -0.1875 to 0.1875
- frozen_out: bfloat16 [1024, 1024], replicated, may hold values from -1.5 to 1.5
- frozen_up: bfloat16 [1024, 4096], replicated, may hold values from -0.1875 to 0.1875
- frozen_down: bfloat16 [4096, 1024], replicated, may hold values from -0.09375 to 0.09375
- frozen_bias: float32 [9216], replicated, may hold values from -0.6 to 0.6
- norm_gain: float32 [3, 1024], replicated, may hold values from 0.5 to 1.5
- norm_shift: float32 [3, 1024], replicated, may hold values from -0.6 to 0.6
- master_matrix: float32 [32, 256, 256], P('vocab'), may hold values from -0.06 to 0.06
- lens_bias: float32 [2, 1024], P(None, 'vocab'), may hold values from -0.6 to 0.6
- matrix_first: float32 [32, 256, 256], P('vocab'), may hold values from -0.2986819 to 0.2986819
- matrix_second: float32 [32, 256, 256], P('vocab'), may hold values from 0.0002048 to 0.0008192
- left_stat: float32 [32, 256, 256], P('vocab'), as said below
- right_stat: float32 [32, 256, 256], P('vocab'), as said below
- left_basis: float32 [32, 256, 256], P('vocab'), may hold values from -1 to 1, as said below
- right_basis: float32 [32, 256, 256], P('vocab'), may hold values from -1 to 1, as said below
- bias_first: float32 [2, 1024], P(None, 'vocab'), may hold values from -0.2986819 to 0.2986819
- bias_second: float32 [2, 1024], P(None, 'vocab'), may hold values from 0.0002048 to 0.0008192
Outputs:
- loss_sum: float32 [], replicated
- loss_count: float32 [], replicated
- new_matrix: float32 [32, 256, 256], P('vocab')
- new_first: float32 [32, 256, 256], P('vocab')
- new_second: float32 [32, 256, 256], P('vocab')
- new_left: float32 [32, 256, 256], P('vocab')
- new_right: float32 [32, 256, 256], P('vocab')
- renewed_left_basis: float32 [32, 256, 256], P('vocab')
- new_rbasis: float32 [32, 256, 256], P('vocab')
- new_bias: float32 [2, 1024], P(None, 'vocab')
- new_bias_first: float32 [2, 1024], P(None, 'vocab')
- new_bias_second: float32 [2, 1024], P(None, 'vocab')
Inputs may be any that keep to these rules, and one draw needn't show every extreme that they name: `lengths`: each row sums to 1024, and its largest entry is exactly 512. `owners`: each block number appears once. `left_stat`: each block symmetric positive definite. `right_stat`: each block symmetric positive definite. `left_basis`: each block orthogonal. `right_basis`: each block orthogonal.
All inputs are finite; a program needn't handle non-finite values.
Results may differ from a plain program's by a relative error of at most 0.034.
Values may be sent and summed in bfloat16 or wider, within the bound.
No kernel may reach another device: no remote copies, remote signals or barrier semaphores. Data moves between devices by JAX's collectives and lax.ppermute only.
A program may use at most 576 MiB of HBM per device.

v0:
```python
import jax
import jax.numpy as jnp
from jax import lax
from jax.sharding import PartitionSpec as P

HEADS = 16
HEAD_DIM = 64
ROT = 16
BS = 256
STEP = 5


HIGHEST = lax.Precision.HIGHEST
NORM_EPS = 1e-05
BETA_ONE = 0.9
BETA_TWO = 0.999
BETA_STAT = 0.95
ADAM_EPS = 1e-08
MATRIX_RATE = 0.01
BIAS_RATE = 0.1
DECAY = 0.1
MASKED = -1e30


def matmul(left, right):
    return jnp.dot(left, right, precision=HIGHEST, preferred_element_type=jnp.float32)


def layer_norm(values, gain_row, shift_row):
    centred = values - jnp.mean(values, -1, keepdims=True)
    spread = jnp.mean(centred * centred, -1, keepdims=True)
    return centred * lax.rsqrt(spread + NORM_EPS) * gain_row + shift_row


def places(index, seq_lens):
    ends = jnp.cumsum(seq_lens)
    segment = jnp.sum((index[:, None] >= ends[None, :]).astype(jnp.int32), 1)
    starts = ends - seq_lens
    picked = segment[:, None] == jnp.arange(seq_lens.shape[0], dtype=jnp.int32)[None, :]
    offset = jnp.sum(jnp.where(picked, starts[None, :], 0), 1)
    return (segment, index - offset)


def rotate(heads_in, position):
    half = ROT // 2
    freq = 10000.0 ** (-2.0 * jnp.arange(half, dtype=jnp.float32) / ROT)
    angle = position.astype(jnp.float32)[:, None] * freq[None, :]
    cosine = jnp.cos(angle)[:, None, :]
    sine = jnp.sin(angle)[:, None, :]
    first_half = heads_in[..., :half]
    second_half = heads_in[..., half:ROT]
    return jnp.concatenate(
        [
            first_half * cosine - second_half * sine,
            second_half * cosine + first_half * sine,
            heads_in[..., ROT:],
        ],
        -1,
    )


def partial_sums(logits, highest):
    shifted = jnp.exp(logits - highest[..., None])
    sums = jnp.sum(shifted, -1)
    cross = jnp.sum(shifted[..., :1, :] * (logits[..., :1, :] - logits[..., 1:, :]), -1)
    return (sums, cross)


def orthonormal(columns):
    gram = matmul(columns.T, columns)
    factor = jnp.linalg.cholesky(gram)
    return lax.linalg.triangular_solve(
        factor, columns, left_side=False, lower=True, transpose_a=True
    )


def soap(weight, grad, first, second, left, right, lbase, rbase):
    rotated = matmul(matmul(lbase.T, grad), rbase)
    first_new = BETA_ONE * first + (1.0 - BETA_ONE) * grad
    second_new = BETA_TWO * second + (1.0 - BETA_TWO) * rotated * rotated
    moment_rot = matmul(matmul(lbase.T, first_new), rbase)
    scaled = (
        moment_rot
        / (1.0 - BETA_ONE**STEP)
        / (jnp.sqrt(second_new / (1.0 - BETA_TWO**STEP)) + ADAM_EPS)
    )
    update = matmul(matmul(lbase, scaled), rbase.T)
    weight_new = weight - MATRIX_RATE * (update + DECAY * weight)
    left_new = BETA_STAT * left + (1.0 - BETA_STAT) * matmul(grad, grad.T)
    right_new = BETA_STAT * right + (1.0 - BETA_STAT) * matmul(grad.T, grad)
    return (
        weight_new,
        first_new,
        second_new,
        left_new,
        right_new,
        orthonormal(matmul(left_new, lbase)),
        orthonormal(matmul(right_new, rbase)),
    )


def adam_bias(bias, grad, first, second):
    first_new = BETA_ONE * first + (1.0 - BETA_ONE) * grad
    second_new = BETA_TWO * second + (1.0 - BETA_TWO) * grad * grad
    scaled = (
        first_new
        / (1.0 - BETA_ONE**STEP)
        / (jnp.sqrt(second_new / (1.0 - BETA_TWO**STEP)) + ADAM_EPS)
    )
    return (bias - BIAS_RATE * scaled, first_new, second_new)


def slope_terms(part_logits, part_norms, partition_count):
    target = jnp.exp(part_logits[:, :1] - part_norms[:, :1, None])
    probes = jnp.exp(part_logits[:, 1:] - part_norms[:, 1:, None])
    return (partition_count[:, None, None] * (probes - target)).astype(jnp.bfloat16)


def body(
    tokens,
    loss_position_mask,
    lengths,
    owners,
    embed_in,
    unembedding_table,
    frozen_qkv,
    frozen_out,
    frozen_up,
    frozen_down,
    frozen_bias,
    norm_gain,
    norm_shift,
    master_matrix,
    lens_bias,
    matrix_first,
    matrix_second,
    left_stat,
    right_stat,
    left_basis,
    right_basis,
    bias_first,
    bias_second,
):
    width = embed_in.shape[1]
    shards = lax.axis_size("vocab")
    where = lax.axis_index("vocab")
    group = tokens.shape[0]
    own = group // shards
    units = frozen_up.shape[1]
    nblk = width // BS
    gathered, biases = (
        lax.all_gather(master_matrix, "vocab", axis=0, tiled=True),
        lax.all_gather(lens_bias, "vocab", axis=1, tiled=True),
    )
    order = jnp.argsort(owners)
    matrices = (
        jnp.take(gathered, order, axis=0)
        .reshape(2, nblk, nblk, BS, BS)
        .transpose(0, 1, 3, 2, 4)
        .reshape(2, width, width)
    )
    table_rows = embed_in.shape[0]
    local_ids = tokens - where * table_rows
    inside = (local_ids >= 0) & (local_ids < table_rows)
    looked = jnp.take(embed_in, jnp.clip(local_ids, 0, table_rows - 1), axis=0)
    looked = jnp.where(inside[:, None], looked, jnp.zeros((), jnp.bfloat16))
    embedded = lax.psum_scatter(looked, "vocab", scatter_dimension=0, tiled=True).astype(
        jnp.float32
    )
    seq_lens = lengths[0]
    index = where * own + jnp.arange(own, dtype=jnp.int32)
    segment, position = places(index, seq_lens)
    attn_in = layer_norm(embedded, norm_gain[0], norm_shift[0]).astype(jnp.bfloat16)
    mlp_in = layer_norm(embedded, norm_gain[1], norm_shift[1]).astype(jnp.bfloat16)
    projected = (
        jnp.dot(attn_in, frozen_qkv, preferred_element_type=jnp.float32) + frozen_bias[: 3 * width]
    )
    queries = rotate(projected[:, :width].reshape(own, HEADS, HEAD_DIM), position).astype(
        jnp.bfloat16
    )
    keys = rotate(projected[:, width : 2 * width].reshape(own, HEADS, HEAD_DIM), position).astype(
        jnp.bfloat16
    )
    values = projected[:, 2 * width :].astype(jnp.bfloat16)
    key_value = jnp.concatenate([keys.reshape(own, width), values], 1)
    piece = lax.all_gather(key_value, "vocab", axis=0, tiled=True)
    highest = jnp.full((HEADS, own), MASKED, jnp.float32)
    count = piece.shape[0]
    key_index = jnp.arange(count, dtype=jnp.int32)
    key_segment, _ = places(key_index, seq_lens)
    piece_keys = piece[:, :width].reshape(count, HEADS, HEAD_DIM)
    piece_values = piece[:, width:].reshape(count, HEADS, HEAD_DIM)
    attention_scores = jnp.einsum(
        "qhd,khd->hqk", queries, piece_keys, preferred_element_type=jnp.float32
    ) * HEAD_DIM ** (-0.5)
    allowed = (segment[:, None] == key_segment[None, :]) & (key_index[None, :] <= index[:, None])
    attention_scores = jnp.where(allowed[None], attention_scores, MASKED)
    new_high = jnp.maximum(highest, jnp.max(attention_scores, -1))
    weights = jnp.where(allowed[None], jnp.exp(attention_scores - new_high[..., None]), 0.0)
    totals = jnp.sum(weights, -1)
    accum = jnp.einsum(
        "hqk,khd->hqd",
        weights.astype(jnp.bfloat16),
        piece_values,
        preferred_element_type=jnp.float32,
    )
    highest, totals, accum = (new_high, totals, accum)
    mixed = (
        jnp.transpose(accum / totals[..., None], (1, 0, 2)).reshape(own, width).astype(jnp.bfloat16)
    )
    attn_out = (
        jnp.dot(mixed, frozen_out, preferred_element_type=jnp.float32)
        + frozen_bias[3 * width : 4 * width]
    )
    activ = jax.nn.gelu(
        jnp.dot(mlp_in, frozen_up, preferred_element_type=jnp.float32)
        + frozen_bias[4 * width : 4 * width + units],
        approximate=False,
    ).astype(jnp.bfloat16)
    layer_out = (
        embedded
        + attn_out
        + (
            jnp.dot(activ, frozen_down, preferred_element_type=jnp.float32)
            + frozen_bias[4 * width + units :]
        )
    )

    def final_norm(values_in):
        return layer_norm(values_in, norm_gain[2], norm_shift[2])

    sources = (embedded.astype(jnp.bfloat16), layer_out.astype(jnp.bfloat16))
    residual = (embedded, layer_out)
    normed = [final_norm(layer_out).astype(jnp.bfloat16)]
    pulls = []
    for which in range(2):
        product = jnp.dot(
            sources[which], matrices[which].astype(jnp.bfloat16), preferred_element_type=jnp.float32
        )
        lensed = residual[which] + product + biases[which]
        normed_out, pull = jax.vjp(final_norm, lensed)
        normed.append(normed_out.astype(jnp.bfloat16))
        pulls.append(pull)
    counted = loss_position_mask.astype(jnp.float32)
    vocab_cols = unembedding_table.shape[0]
    every = lax.all_gather(jnp.stack(normed), "vocab", axis=1, tiled=True)
    size = min(512, group)
    count = group // size
    blocks = every.reshape(3, count, size, width).transpose(1, 0, 2, 3)

    def block_high(normed_blk):
        logits_blk = jnp.einsum(
            "kbd,vd->bkv", normed_blk, unembedding_table, preferred_element_type=jnp.float32
        )
        return (logits_blk, jnp.max(logits_blk, -1))

    logits, highest = lax.map(block_high, blocks)
    highest = lax.pmax(highest.reshape(group, 3), "vocab")

    def block_sums(args):
        return partial_sums(args[0], args[1])

    sums, cross = lax.map(block_sums, (logits, highest.reshape(count, size, 3)))
    logits = logits.reshape(group, 3, vocab_cols)
    sums, cross = lax.psum((sums.reshape(group, 3), cross.reshape(group, 2)), "vocab")
    log_total = highest + jnp.log(sums)
    diverge = cross / sums[:, :1] - log_total[:, :1] + log_total[:, 1:]
    loss_sum, loss_count = lax.psum((jnp.sum(counted[:, None] * diverge), jnp.sum(counted)), "rows")
    loss_slope = slope_terms(logits, log_total, counted)
    dnormed = lax.psum_scatter(
        jnp.einsum(
            "yzq,qa->yza", loss_slope, unembedding_table, preferred_element_type=jnp.float32
        ),
        "vocab",
        scatter_dimension=0,
        tiled=True,
    )
    grads = []
    bias_grads = []
    for which in range(2):
        dlensed = pulls[which](dnormed[:, which])[0]
        bias_grads.append(jnp.sum(dlensed, 0))
        grads.append(
            jnp.einsum(
                "nd,ne->de",
                sources[which],
                dlensed.astype(jnp.bfloat16),
                preferred_element_type=jnp.float32,
            )
        )
    matrix_grad = (
        jnp.stack(grads).reshape(2, nblk, BS, nblk, BS).transpose(0, 1, 3, 2, 4).reshape(-1, BS, BS)
    )
    slot_grad = jnp.take(matrix_grad, owners, axis=0)
    bias_grad = jnp.stack(bias_grads)
    per_dev = master_matrix.shape[0]
    bias_cols = lens_bias.shape[1]
    slot_grad, bias_grad = lax.psum((slot_grad, bias_grad), ("rows", "vocab"))
    slot_grad = lax.dynamic_slice_in_dim(slot_grad, where * per_dev, per_dev, 0)
    bias_grad = lax.dynamic_slice_in_dim(bias_grad, where * bias_cols, bias_cols, 1)
    (
        new_matrix,
        new_first,
        new_second,
        new_left,
        new_right,
        renewed_left_basis,
        new_rbasis,
    ) = jax.vmap(soap)(
        master_matrix,
        slot_grad,
        matrix_first,
        matrix_second,
        left_stat,
        right_stat,
        left_basis,
        right_basis,
    )
    new_bias, new_bias_first, new_bias_second = adam_bias(
        lens_bias, bias_grad, bias_first, bias_second
    )
    return (
        loss_sum,
        loss_count,
        new_matrix,
        new_first,
        new_second,
        new_left,
        new_right,
        renewed_left_basis,
        new_rbasis,
        new_bias,
        new_bias_first,
        new_bias_second,
    )


def solution(mesh):
    in_specs = (
        P("rows"),
        P("rows"),
        P("rows", None),
        P(),
        P("vocab", None),
        P("vocab", None),
        P(),
        P(),
        P(),
        P(),
        P(),
        P(),
        P(),
        P("vocab", None, None),
        P(None, "vocab"),
        P("vocab", None, None),
        P("vocab", None, None),
        P("vocab", None, None),
        P("vocab", None, None),
        P("vocab", None, None),
        P("vocab", None, None),
        P(None, "vocab"),
        P(None, "vocab"),
    )
    out_specs = (
        P(),
        P(),
        P("vocab", None, None),
        P("vocab", None, None),
        P("vocab", None, None),
        P("vocab", None, None),
        P("vocab", None, None),
        P("vocab", None, None),
        P("vocab", None, None),
        P(None, "vocab"),
        P(None, "vocab"),
        P(None, "vocab"),
    )
    return jax.shard_map(body, mesh=mesh, in_specs=in_specs, out_specs=out_specs, check_vma=False)
```

profile of v0, /device:TPU:0, one launch (start us, length us, event | category | flops | bytes accessed | tf_op | source)
XLA Modules:
  0.0 1514.3 jit_solution(4334236825876551917)
XLA Ops:
  8.8 12.4 gather_fusion
  21.2 3.2 select_select_fusion
  27.1 35.9 %reduce-scatter.3.cloned.1.call-done = bf16[128,1024]{1,0:T(8,128)(2,1)} async-done(((bf16[1024,1024]{1,0:T(8,128)(2,1)}), bf16[128,1024]{1,0:T(8,128)(2,1)}) %reduce-scatter.3.cloned.1.call-update) | async-done | bytes 262160 | tf_op jit(solution)/shard_map/reduce_scatter | solution.py:167
  65.8 4.0 convolution_add_fusion.1
  79.7 8.5 all_gather.14
  90.5 12.3 convolution_add_fusion.6
  102.8 8.3 all-gather.6.cloned.1.call-done
  111.1 5.1 gather_fusion.1
  116.1 3.6 select_convert_fusion
  119.7 3.2 copy.271
  128.1 31.0 %all-gather.4.cloned.1.call-done = bf16[1024,2048]{1,0:T(8,128)(2,1)} async-done(((bf16[128,2048]{1,0:T(8,128)(2,1)}), bf16[1024,2048]{1,0:T(8,128)(2,1)}) %all-gather.4.cloned.1.call-update) | async-done | bytes 4194320 | tf_op jit(solution)/shard_map/all_gather | solution.py:186
  159.2 4.7 fusion.194
  163.9 4.0 copy.181
  167.9 4.1 copy.180
  172.0 3.2 fusion.16
  184.8 62.9 %all-gather.8.cloned.1.call-done = bf16[3,1024,1024]{2,1,0:T(8,128)(2,1)} async-done(((bf16[3,128,1024]{2,1,0:T(8,128)(2,1)}), bf16[3,1024,1024]{2,1,0:T(8,128)(2,1)}) %all-gather.8.cloned.1.call-update) | async-done | bytes 6291472 | tf_op jit(solution)/shard_map/all_gather | solution.py:246
  247.7 6.8 copy.270
  254.5 96.7 %while.28 = (s32[]{:T(128)}, f32[2,512,3,6288]{1,3,2,0:T(8,128)}, f32[2,512,3]{1,2,0:T(4,128)S(1)}, bf16[2,3,512,1024]{3,2,1,0:T(8,128)(2,1)}, bf16[6288,1024]{1,0:T(8,128)(2,1)}, /*index=5*/s32[]{:T(128)}) while((s32[]{:T(128)}, f32[2,512,3,6288]{1,3,2,0:T(8,128)}, f32[2,512,3]{1,2,0:T(4,128)S(1)}, bf16[2,3,512,1024]{3,2,1,0:T(8,128)(2,1)}, ...), condition=%wide.region_18.20_spmd, body=%wide.region_16.19_spmd.sunk | while | flops 19789993984 | bytes 131947592 | solution.py:257
  254.6 34.6 %bitcast_dynamic-update-slice_fusion.12 = (f32[2,512,3,6288]{1,3,2,0:T(8,128)}, f32[3,512,6288]{1,2,0:T(8,128)}) fusion(f32[2,512,3,6288]{1,3,2,0:T(8,128)} %get-tuple-element.416, s32[]{:T(128)S(6)} %copy.281, bf16[6288,1024]{1,0:T(8,128)(2,1)} %get-tuple-element.425, bf16[2,3,512,1024]{3,2,1,0:T(8,128)(2,1)} %get-tuple-element.424), kind=kOutput, calls=%fused_computation.3.clone.1 | convolution fusion | flops 19780337664 | bytes 93291520 | tf_op jit(solution)/shard_map/while/body/eval_jaxpr/kbd,vd->bkv/dot_general | solution.py:252
  289.2 13.7 bitcast_reduce_fusion.2
  302.9 34.6 %bitcast_dynamic-update-slice_fusion.12 = (f32[2,512,3,6288]{1,3,2,0:T(8,128)}, f32[3,512,6288]{1,2,0:T(8,128)}) fusion(f32[2,512,3,6288]{1,3,2,0:T(8,128)} %get-tuple-element.416, s32[]{:T(128)S(6)} %copy.281, bf16[6288,1024]{1,0:T(8,128)(2,1)} %get-tuple-element.425, bf16[2,3,512,1024]{3,2,1,0:T(8,128)(2,1)} %get-tuple-element.424), kind=kOutput, calls=%fused_computation.3.clone.1 | convolution fusion | flops 19780337664 | bytes 93291520 | tf_op jit(solution)/shard_map/while/body/eval_jaxpr/kbd,vd->bkv/dot_general | solution.py:252
  337.5 13.7 bitcast_reduce_fusion.2
  351.3 26.7 %pmax.7 = f32[1024,3]{0,1:T(4,128)S(1)} all-reduce(f32[1024,3]{0,1:T(4,128)S(1)} %bitcast.263), channel_id=1, replica_groups=mesh['rows'=4,'vocab'=8] {'vocab'}, use_global_device_ids=true, to_apply=%region_19.21 | all-reduce | flops 3072 | bytes 24576 | tf_op jit(solution)/shard_map/pmax | solution.py:258
  377.9 129.1 %while.29 = (s32[]{:T(128)}, f32[2,512,3]{1,2,0:T(4,128)S(1)}, f32[2,512,2]{1,2,0:T(2,128)S(1)}, f32[2,512,3,6288]{1,3,2,0:T(8,128)}, f32[2,512,3]{1,2,0:T(4,128)S(1)}, /*index=5*/s32[]{:T(128)}) while((s32[]{:T(128)}, f32[2,512,3]{1,2,0:T(4,128)S(1)}, f32[2,512,2]{1,2,0:T(2,128)S(1)}, f32[2,512,3,6288]{1,3,2,0:T(8,128)}, ...), condition=%wide.region_23.25_spmd, body=%wide.region_20.24_spmd.sunk | while | flops 38630912 | bytes 218976352 | solution.py:263
  378.0 36.8 %fusion.252 = (f32[512,3]{0,1:T(4,128)S(1)}, f32[512,3,6288]{0,2,1:T(8,128)}, f32[512,3,6288]{0,2,1:T(8,128)}) fusion(f32[512,3]{0,1:T(4,128)S(1)} %dynamic-slice_bitcast_fusion.4, f32[2,512,3,6288]{1,3,2,0:T(8,128)} %get-tuple-element.442, s32[]{:T(128)S(6)} %copy.290), kind=kLoop, calls=%fused_computation.323.clone.1 | loop fusion | flops 19315200 | bytes 115912704 | tf_op jit(solution)/shard_map/while/body/eval_jaxpr/reduce_sum | solution.py:64
  414.8 14.5 slice_bitcast_fusion.13
  429.3 13.2 fusion.253
  442.5 36.8 %fusion.252 = (f32[512,3]{0,1:T(4,128)S(1)}, f32[512,3,6288]{0,2,1:T(8,128)}, f32[512,3,6288]{0,2,1:T(8,128)}) fusion(f32[512,3]{0,1:T(4,128)S(1)} %dynamic-slice_bitcast_fusion.4, f32[2,512,3,6288]{1,3,2,0:T(8,128)} %get-tuple-element.442, s32[]{:T(128)S(6)} %copy.290), kind=kLoop, calls=%fused_computation.323.clone.1 | loop fusion | flops 19315200 | bytes 115912704 | tf_op jit(solution)/shard_map/while/body/eval_jaxpr/reduce_sum | solution.py:64
  479.3 14.5 slice_bitcast_fusion.13
  493.9 13.2 fusion.253
  507.0 26.0 %all-reduce.1 = (f32[1024,2]{0,1:T(2,128)S(1)}, f32[1024,3]{0,1:T(4,128)S(1)}) all-reduce(f32[1024,2]{0,1:T(2,128)S(1)} %bitcast.273, f32[1024,3]{0,1:T(4,128)S(1)} %bitcast.264), channel_id=1, replica_groups=mesh['rows'=4,'vocab'=8] {'vocab'}, use_global_device_ids=true, to_apply=%region_24.26 | all-reduce | flops 5120 | bytes 40960 | tf_op jit(solution)/shard_map/psum | solution.py:265
  533.1 74.9 %copy.185 = f32[2,512,3,6288]{3,1,0,2:T(8,128)} copy(f32[2,512,3,6288]{1,3,2,0:T(8,128)} %get-tuple-element.430) | data formatting | bytes 154533888 | tf_op jit(solution)/shard_map/while | solution.py:257
  608.0 18.3 %fusion.12 = f32[1024,6288]{1,0:T(8,128)} fusion(f32[1024,3,6288]{2,0,1:T(8,128)} %bitcast.44, f32[1024]{0:T(1024)S(1)} %bitcast.265), kind=kLoop, calls=%fused_computation.32 | loop fusion | flops 6438912 | bytes 51515392 | tf_op jit(solution)/shard_map/sub | solution.py:116
  626.9 39.9 %fusion.13 = f32[1024,2,1024]{2,0,1:T(8,128)} fusion(f32[1024,3,6288]{2,0,1:T(8,128)} %bitcast.44, f32[1024,6288]{1,0:T(8,128)} %fusion.12, f32[1024,2]{0,1:T(2,128)S(1)} %get-tuple-element.242, f32[1024]{0:T(1024)S(1)} %copy-done.35, bf16[6288,1024]{1,0:T(8,128)(2,1)} %get-tuple-element.501), kind=kOutput, calls=%fused_computation.33 | convolution fusion | flops 26425294848 | bytes 99921920 | tf_op jit(solution)/shard_map/yzq,qa->yza/dot_general | solution.py:271
  667.5 87.6 %reduce-scatter.5.cloned.1.call-done = f32[128,2,1024]{2,0,1:T(8,128)} async-done(((f32[1024,2,1024]{2,0,1:T(8,128)}), f32[128,2,1024]{2,0,1:T(8,128)}) %reduce-scatter.5.cloned.1.call-update) | async-done | bytes 1048592 | tf_op jit(solution)/shard_map/reduce_scatter | solution.py:270
  758.3 2.7 fusion.106
  761.0 6.1 stack.35
  767.1 4.9 copy.188
  772.0 2.7 fusion.105
  774.8 5.6 stack.34
  780.4 3.1 copy.187
  783.9 3.8 pad_maximum_fusion
  787.7 7.7 gather_fusion.2
  795.3 9.0 copy.189
  804.3 7.8 broadcast_select_fusion
  818.0 10.9 all-reduce.2
  829.2 38.6 %psum.47 = f32[2,1024]{1,0:T(2,128)S(1)} all-reduce(f32[2,1024]{1,0:T(2,128)S(1)} %pad_maximum_fusion.6), channel_id=1, replica_groups=mesh['rows'=4,'vocab'=8] {'rows','vocab'}, use_global_device_ids=true, to_apply=%region_42.46 | all-reduce | flops 2048 | bytes 16384 | tf_op jit(solution)/shard_map/psum | solution.py:298
  868.4 121.9 %all-reduce.5.cloned.1.call-done = f32[32,256,256]{1,2,0:T(8,128)} async-done(((f32[32,256,256]{1,2,0:T(8,128)}), f32[32,256,256]{1,2,0:T(8,128)}) %all-reduce.5.cloned.1.call-update) | async-done | bytes 8388624 | tf_op jit(solution)/shard_map/psum | solution.py:298
  995.2 3.1 fusion.87
  1007.2 3.9 fusion.33
  1012.5 2.9 fusion.32
  1023.1 46.9 %custom-call.21 = f32[4,128,128]{2,1,0:T(8,128)S(1)} custom-call(f32[4,128,128]{2,1,0:T(8,128)S(1)} %cholesky.201), custom_call_target="Cholesky" | custom-call | tf_op jit(solution)/shard_map/vmap(jit(cholesky))/cholesky | solution.py:71
  1075.6 47.9 %custom-call.17 = f32[4,128,128]{2,1,0:T(8,128)} custom-call(f32[4,128,128]{2,1,0:T(8,128)S(1)} %cholesky.198), custom_call_target="Cholesky" | custom-call | tf_op jit(solution)/shard_map/vmap(jit(cholesky))/cholesky | solution.py:71
  1125.4 40.7 %custom-call.22 = f32[4,1,128,128]{2,3,1,0:T(8,128)} custom-call(f32[4,1,128,128]{3,2,1,0:T(8,128)} %get-tuple-element.240), custom_call_target="InvertDiagBlocksLowerTriangular" | custom-call | tf_op jit(solution)/shard_map/vmap(jit(cholesky))/cholesky | solution.py:71
  1169.9 48.4 %custom-call.23 = f32[4,128,128]{2,1,0:T(8,128)} custom-call(f32[4,128,128]{2,1,0:T(8,128)} %convolution_subtract_fusion.2), custom_call_target="Cholesky" | custom-call | tf_op jit(solution)/shard_map/vmap(jit(cholesky))/cholesky | solution.py:71
  1220.3 40.9 %custom-call.18 = f32[4,1,128,128]{2,3,1,0:T(8,128)} custom-call(f32[4,1,128,128]{3,2,1,0:T(8,128)} %get-tuple-element.241), custom_call_target="InvertDiagBlocksLowerTriangular" | custom-call | tf_op jit(solution)/shard_map/vmap(jit(cholesky))/cholesky | solution.py:71
  1265.6 48.3 %custom-call.19 = f32[4,128,128]{2,1,0:T(8,128)} custom-call(f32[4,128,128]{2,1,0:T(8,128)} %convolution_subtract_fusion.3), custom_call_target="Cholesky" | custom-call | tf_op jit(solution)/shard_map/vmap(jit(cholesky))/cholesky | solution.py:71
  1316.8 2.8 select_select_fusion.1
  1320.6 5.5 while.30
  1326.0 80.2 %custom-call.20 = f32[4,2,128,128]{2,3,1,0:T(8,128)} custom-call(f32[4,2,128,128]{3,2,1,0:T(8,128)} %bitcast.254), custom_call_target="InvertDiagBlocksLowerTriangular" | custom-call | tf_op jit(solution)/shard_map/vmap()/triangular_solve/custom-call.0 | solution.py:72
  1412.7 7.7 while.31
  1413.4 3.2 bitcast_dynamic-update-slice_fusion.17
  1417.3 3.1 bitcast_dynamic-update-slice_fusion.17
  1420.4 80.2 %custom-call.24 = f32[4,2,128,128]{2,3,1,0:T(8,128)} custom-call(f32[4,2,128,128]{3,2,1,0:T(8,128)} %bitcast.63), custom_call_target="InvertDiagBlocksLowerTriangular" | custom-call | tf_op jit(solution)/shard_map/vmap()/triangular_solve/custom-call.0 | solution.py:72
  (292 shorter events, 109.0 us)
Async XLA Ops:
  7.2 173.2 %copy-start = (bf16[1024,1024]{1,0:T(8,128)(2,1)S(1)}, bf16[1024,1024]{1,0:T(8,128)(2,1)}, u32[]{:S(2)}) copy-start(bf16[1024,1024]{1,0:T(8,128)(2,1)} %param.39) | copy-start | bytes 6291460
  7.2 55.8 %reduce-scatter.3.cloned.1.call-start = ((), (), s32[]{:S(2)}) async-start(), calls=%async_computation.2 | async-start | bytes 2359296 | tf_op jit(solution)/shard_map/reduce_scatter | solution.py:167
  21.1 3.3 copy-start.18
  21.1 4.2 copy-start.62
  21.1 4.7 copy-start.40
  21.1 5.3 copy-start.41
  21.1 44.6 %slice-start = ((f32[9216]{0:T(1024)}), f32[3072]{0:T(1024)S(1)}, s32[]{:S(2)}) async-start(f32[9216]{0:T(1024)} %param.42), calls=%async_computation.8 | async-start | bytes 24576 | tf_op jit(solution)/shard_map/slice | solution.py:176
  24.4 86.7 %all-gather.6.cloned.1.call-start = ((), (), s32[]{:S(2)}) async-start(), calls=%async_computation.4 | async-start | bytes 4718592 | tf_op jit(solution)/shard_map/all_gather | solution.py:152
  25.3 133.9 %all-gather.4.cloned.1.call-start = ((), (), s32[]{:S(2)}) async-start(), calls=%async_computation.3 | async-start | bytes 4718592 | tf_op jit(solution)/shard_map/all_gather | solution.py:186
  25.6 39.7 %copy-start.56 = (s32[128]{0:T(128)}, s32[128]{0:T(128)S(1)}, u32[]{:S(2)}) copy-start(s32[128]{0:T(128)S(1)} %iota_add_fusion) | copy-start | bytes 1540
  25.6 39.6 %copy-start.57 = (s32[128]{0:T(128)}, s32[128]{0:T(128)S(1)}, u32[]{:S(2)}) copy-start(s32[128]{0:T(128)S(1)} %convert_reduce_fusion.2) | copy-start | bytes 1540
  27.1 155.6 %copy-start.31 = (f32[1,1024]{1,0:T(1,128)}, f32[1,1024]{1,0:T(1,128)S(1)}, u32[]{:S(2)}) copy-start(f32[1,1024]{1,0:T(1,128)S(1)} %get-tuple-element.244) | copy-start | bytes 12292
  69.7 8.3 copy-start.33
  69.8 8.3 copy-start.63
  69.8 9.9 copy-start.47
  70.5 20.0 %copy-start.10 = (bf16[128,1024]{1,0:T(8,128)(2,1)S(1)}, bf16[128,1024]{1,0:T(8,128)(2,1)}, u32[]{:S(2)}) copy-start(bf16[128,1024]{1,0:T(8,128)(2,1)} %reduce-scatter.3.cloned.1.call-done) | copy-start | bytes 786436
  78.0 169.7 %all-gather.8.cloned.1.call-start = ((), (), s32[]{:S(2)}) async-start(), calls=%async_computation.5 | async-start | bytes 7077888 | tf_op jit(solution)/shard_map/all_gather | solution.py:246
  124.5 2.3 copy-start.34
  127.4 55.4 %copy-start.4 = (f32[128,1024]{1,0:T(8,128)}, f32[128,1024]{1,0:T(8,128)S(1)}, u32[]{:S(2)}) copy-start(f32[128,1024]{1,0:T(8,128)S(1)} %get-tuple-element.266) | copy-start | bytes 1572868
  127.4 36.5 %copy-start.43 = (f32[128]{0:T(128)}, f32[128]{0:T(128)S(1)}, u32[]{:S(2)}) copy-start(f32[128]{0:T(128)S(1)} %broadcast_multiply_fusion.1) | copy-start | bytes 1540
  127.6 36.3 %copy-start.58 = (f32[128]{0:T(128)}, f32[128]{0:T(128)S(1)}, u32[]{:S(2)}) copy-start(f32[128]{0:T(128)S(1)} %multiply_reduce_fusion.3) | copy-start | bytes 1540
  163.9 8.1 copy-start.27
  163.9 8.2 copy-start.29
  163.9 8.2 copy-start.30
  175.2 2.5 copy-start.23
  177.8 2.6 copy-start.28
  180.3 1.6 copy-start.14
  180.3 2.4 copy-start.44
  180.3 2.4 copy-start.49
  180.9 2.1 copy-start.8
  181.9 2.2 copy-start.36
  182.4 72.1 %copy-start.6 = (f32[128,1024]{1,0:T(8,128)}, f32[128,1024]{1,0:T(8,128)S(1)}, u32[]{:S(2)}) copy-start(f32[128,1024]{1,0:T(8,128)S(1)} %get-tuple-element.268) | copy-start | bytes 1572868
  182.5 72.0 %copy-start.38 = (f32[128]{0:T(128)}, f32[128]{0:T(128)S(1)}, u32[]{:S(2)}) copy-start(f32[128]{0:T(128)S(1)} %get-tuple-element.274) | copy-start | bytes 1540
  182.7 71.8 %copy-start.60 = (f32[128]{0:T(128)}, f32[128]{0:T(128)S(1)}, u32[]{:S(2)}) copy-start(f32[128]{0:T(128)S(1)} %multiply_reduce_fusion.2) | copy-start | bytes 1540
  182.7 71.8 %copy-start.51 = (f32[128]{0:T(128)}, f32[128]{0:T(128)S(1)}, u32[]{:S(2)}) copy-start(f32[128]{0:T(128)S(1)} %fusion.152) | copy-start | bytes 1540
  184.1 571.0 %reduce-scatter.5.cloned.1.call-start = ((), (), s32[]{:S(2)}) async-start(), calls=%async_computation.6 | async-start | bytes 9437184 | tf_op jit(solution)/shard_map/reduce_scatter | solution.py:270
  254.5 123.4 %copy-start.42 = (f32[2,512,2]{1,2,0:T(2,128)S(1)}, f32[2,512,2]{1,2,0:T(2,128)}, u32[]{:S(2)}) copy-start(f32[2,512,2]{1,2,0:T(2,128)} %custom-call.32) | copy-start | bytes 24580
  608.0 18.3 %copy-start.35 = (f32[1024]{0:T(1024)S(1)}, f32[1024]{0:T(1024)}, u32[]{:S(2)}) copy-start(f32[1024]{0:T(1024)} %convert_element_type.75) | copy-start | bytes 12292
  666.8 88.3 %copy-start.5 = (f32[128,1024]{1,0:T(8,128)S(1)}, f32[128,1024]{1,0:T(8,128)}, u32[]{:S(2)}) copy-start(f32[128,1024]{1,0:T(8,128)} %copy-done.4) | copy-start | bytes 1572868
  666.8 88.3 %copy-start.7 = (f32[128,1024]{1,0:T(8,128)S(1)}, f32[128,1024]{1,0:T(8,128)}, u32[]{:S(2)}) copy-start(f32[128,1024]{1,0:T(8,128)} %copy-done.6) | copy-start | bytes 1572868
  666.8 88.3 %copy-start.32 = (f32[1,1024]{1,0:T(1,128)S(1)}, f32[1,1024]{1,0:T(1,128)}, u32[]{:S(2)}) copy-start(f32[1,1024]{1,0:T(1,128)} %copy-done.31) | copy-start | bytes 12292
  666.8 88.3 %copy-start.39 = (f32[128]{0:T(128)S(1)}, f32[128]{0:T(128)}, u32[]{:S(2)}) copy-start(f32[128]{0:T(128)} %copy-done.38) | copy-start | bytes 1540
  666.9 88.3 %copy-start.45 = (f32[128]{0:T(128)S(1)}, f32[128]{0:T(128)}, u32[]{:S(2)}) copy-start(f32[128]{0:T(128)} %copy-done.43) | copy-start | bytes 1540
  666.9 89.7 %copy-start.59 = (f32[128]{0:T(128)S(1)}, f32[128]{0:T(128)}, u32[]{:S(2)}) copy-start(f32[128]{0:T(128)} %copy-done.58) | copy-start | bytes 1540
  666.9 89.7 %copy-start.61 = (f32[128]{0:T(128)S(1)}, f32[128]{0:T(128)}, u32[]{:S(2)}) copy-start(f32[128]{0:T(128)} %copy-done.60) | copy-start | bytes 1540
  666.9 89.8 %copy-start.50 = (f32[128]{0:T(128)S(1)}, f32[128]{0:T(128)}, u32[]{:S(2)}) copy-start(f32[128]{0:T(128)} %fusion.151) | copy-start | bytes 1540
  666.9 89.8 %copy-start.52 = (f32[128]{0:T(128)S(1)}, f32[128]{0:T(128)}, u32[]{:S(2)}) copy-start(f32[128]{0:T(128)} %copy-done.51) | copy-start | bytes 1540
  666.9 91.3 %copy-start.9 = (f32[128,1024]{1,0:T(8,128)S(1)}, f32[128,1024]{1,0:T(8,128)}, u32[]{:S(2)}) copy-start(f32[128,1024]{1,0:T(8,128)} %copy-done.8) | copy-start | bytes 1572868
  667.0 323.3 %all-reduce.5.cloned.1.call-start = ((), (), s32[]{:S(2)}) async-start(), calls=%async_computation.7 | async-start | bytes 16777216 | tf_op jit(solution)/shard_map/psum | solution.py:298
  767.1 4.9 copy-start.11
  780.4 3.4 copy-start.3
  813.3 4.0 copy-start.37
  813.4 54.4 %copy-start.48 = (f32[2,128]{1,0:T(2,128)S(1)}, f32[2,128]{1,0:T(2,128)}, u32[]{:S(2)}) copy-start(f32[2,128]{1,0:T(2,128)} %param.46) | copy-start | bytes 3076
  813.4 54.4 %copy-start.54 = (f32[2,128]{1,0:T(2,128)S(1)}, f32[2,128]{1,0:T(2,128)}, u32[]{:S(2)}) copy-start(f32[2,128]{1,0:T(2,128)} %param.53) | copy-start | bytes 3076
  813.4 54.4 %copy-start.55 = (f32[2,128]{1,0:T(2,128)S(1)}, f32[2,128]{1,0:T(2,128)}, u32[]{:S(2)}) copy-start(f32[2,128]{1,0:T(2,128)} %param.54) | copy-start | bytes 3076
  814.7 178.7 %copy-start.2 = (f32[4,256,256]{2,1,0:T(8,128)S(1)}, f32[4,256,256]{2,1,0:T(8,128)}, u32[]{:S(2)}) copy-start(f32[4,256,256]{2,1,0:T(8,128)} %param.51) | copy-start | bytes 3145732
  992.0 6.3 copy-start.12
  993.3 5.0 copy-start.25
  999.6 2.7 copy-start.26
  999.6 2.7 copy-start.20
  1004.6 7.9 copy-start.24
  1007.2 9.2 copy-start.13
  1011.1 6.5 copy-start.15
  1420.4 86.8 %copy-start.1 = (bf16[1024,1024]{1,0:T(8,128)(2,1)S(1)}, bf16[1024,1024]{1,0:T(8,128)(2,1)}, u32[]{:S(2)}) copy-start(bf16[1024,1024]{1,0:T(8,128)(2,1)} %param.39) | copy-start | bytes 6291460
  (8 other events, 7.5 us)
Sparse Core Ops, SparseCore 0:
  24.5 38.4 reduce-scatter.2
  65.2 45.8 all-gather.5
  113.2 45.8 all-gather.3
  184.2 63.4 all-gather.7
  667.1 87.9 reduce-scatter.4
  812.3 177.9 all-reduce.4
where the time goes:
time: 1520 us; the launch traced here: 1510 us
  other arithmetic  632 us (42%)
  waiting for transfers between devices  348 us (23%)
  local copies, waits for them, and re-layouts  228 us (15%)
  matrix products  180 us (12%)
  blocking collectives  111 us (7%)
  between operations  15.6 us (1%)
    another operation x16, other arithmetic, orthonormal(): factor = jnp.linalg.cholesky(gram)  277 us
    another operation x7, other arithmetic, orthonormal(): lax.linalg.triangular_solve(factor, columns, left_side=False, lower=True,...  163 us
    psum x1, waiting for transfers between devices, body(): slot_grad, bias_grad = lax.psum((slot_grad, bias_grad), ('rows', 'vocab'))  122 us
    reduce_scatter x1, waiting for transfers between devices, body(): lax.psum_scatter(jnp.einsum('yzq,qa->yza', loss_slope, unembedding_table,...  87.6 us
    while x1, local copies, waits for them, and re-layouts, body(): logits, highest = lax.map(block_high, blocks)  74.9 us
    reduce_sum x2, other arithmetic, partial_sums(): sums = jnp.sum(shifted, -1)  73.6 us
    dot_general x2, matrix products, block_high(): jnp.einsum('kbd,vd->bkv', normed_blk, unembedding_table, preferred_elemen...  69.2 us
    all_gather x1, waiting for transfers between devices, body(): every = lax.all_gather(jnp.stack(normed), 'vocab', axis=1, tiled=True)  62.9 us
  transfers between devices with their start and end apart: 6, of which 6 were waited for; matrix products, arithmetic and copies ran while one was open for 4% of the time, Pallas kernels for 0%

commit v1 on v0

v1 whole, which is shorter than its diff:
```python
import functools

import jax
import jax.numpy as jnp
import numpy as np
from jax import lax
from jax.experimental import pallas as pl
from jax.experimental.pallas import tpu as pltpu
from jax.sharding import PartitionSpec as P

HEADS = 16
HEAD_DIM = 64
ROT = 16
BS = 256
STEP = 5

HIGHEST = lax.Precision.HIGHEST
NORM_EPS = 1e-05
BETA_ONE = 0.9
BETA_TWO = 0.999
BETA_STAT = 0.95
ADAM_EPS = 1e-08
MATRIX_RATE = 0.01
BIAS_RATE = 0.1
DECAY = 0.1
MASKED = -1e30
NB = 64
PIV = 2
VMEM_LIMIT = 56 * 2**20


def _mm(a,b,dims):
    return lax.dot_general(a,b,(dims,((),())),precision=HIGHEST,preferred_element_type=jnp.float32)
def mm_nn(a,b): return _mm(a,b,((1,),(0,)))
def mm_tn(a,b): return _mm(a,b,((0,),(0,)))
def mm_nt(a,b): return _mm(a,b,((1,),(1,)))
def _mb(a,b,dims):
    return lax.dot_general(a.astype(jnp.bfloat16),b.astype(jnp.bfloat16),(dims,((),())),preferred_element_type=jnp.float32)

def eliminate(rows, nb):
    rows=list(rows)
    def pick(i,c):
        return jnp.broadcast_to(rows[i][:,c:c+1],rows[i].shape)
    for j in range(0,nb,PIV):
        low=[[None]*PIV for _ in range(PIV)]
        roots=[None]*PIV
        inv=[[None]*PIV for _ in range(PIV)]
        cur=[[pick(j+p,j+q) if q<=p else None for q in range(PIV)] for p in range(PIV)]
        for q in range(PIV):
            guess=lax.rsqrt(cur[q][q])
            roots[q]=guess*(1.5-0.5*(cur[q][q]*guess)*guess)
            for p in range(q+1,PIV):
                low[p][q]=cur[p][q]*roots[q]
            for p in range(q+1,PIV):
                for t in range(q+1,p+1):
                    cur[p][t]=cur[p][t]-low[p][q]*low[t][q]
        lead=[]
        for p in range(PIV):
            acc=rows[j+p]
            for q in range(p):
                acc=acc-low[p][q]*lead[q]
            lead.append(acc*roots[p])
        back=[None]*PIV
        for p in reversed(range(PIV)):
            acc=lead[p]
            for q in range(p+1,PIV):
                acc=acc-low[q][p]*back[q]
            back[p]=acc*roots[p]
        for i in range(j+PIV,nb):
            cols=[pick(i,j+p) for p in range(PIV)]
            t=cols[0]*back[0]
            for p in range(1,PIV):
                t=t+cols[p]*back[p]
            rows[i]=rows[i]-t
        for p in range(PIV):
            rows[j+p]=lead[p]
    return rows

def soap_kernel(per, where_ref, w_ref,g_ref,first_ref,second_ref,left_ref,right_ref,lb_ref,rb_ref,
                nw_ref,nf_ref,ns_ref,nl_ref,nr_ref,ql_ref,qr_ref,work,prods,stage):
    xor=where_ref[0]
    nm=2*per
    nn=((1,),(0,)); tn=((0,),(0,)); nt=((1,),(1,))
    def slot(s,c):
        g=g_ref[s^xor].astype(jnp.float32)
        gb=g.astype(jnp.bfloat16)
        lb=lb_ref[s]; rb=rb_ref[s]
        lbb=lb.astype(jnp.bfloat16); rbb=rb.astype(jnp.bfloat16)
        rotated=_mb(_mb(lbb,gb,tn),rbb,nn)
        first=BETA_ONE*first_ref[s]+(1.0-BETA_ONE)*g
        second=BETA_TWO*second_ref[s]+(1.0-BETA_TWO)*rotated*rotated
        nf_ref[s]=first; ns_ref[s]=second
        moment=_mb(_mb(lbb,first,tn),rbb,nn)
        scaled=moment/(1.0-BETA_ONE**STEP)/(jnp.sqrt(second/(1.0-BETA_TWO**STEP))+ADAM_EPS)
        update=_mb(_mb(lbb,scaled,nn),rbb,nt)
        w=w_ref[s]
        nw_ref[s]=w-MATRIX_RATE*(update+DECAY*w)
        nl=BETA_STAT*left_ref[s]+(1.0-BETA_STAT)*_mb(gb,gb,nt)
        nr=BETA_STAT*right_ref[s]+(1.0-BETA_STAT)*_mb(gb,gb,tn)
        nl_ref[s]=nl; nr_ref[s]=nr
        pl_=mm_nn(nl,lb); pr_=mm_nn(nr,rb)
        prods[s]=pl_; prods[per+s]=pr_
        work[s]=mm_tn(pl_,pl_); work[per+s]=mm_tn(pr_,pr_)
        return c
    lax.fori_loop(0,per,slot,0,unroll=True)
    lane=lax.broadcasted_iota(jnp.int32,(NB,128),1)
    row=lax.broadcasted_iota(jnp.int32,(NB,128),0)
    ident=(lane==row+NB).astype(jnp.float32)
    idrow=lax.broadcasted_iota(jnp.int32,(NB,BS),0)
    col=lax.broadcasted_iota(jnp.int32,(NB,BS),1)
    colw=lax.broadcasted_iota(jnp.int32,(BS,BS),1)
    upper=lax.broadcasted_iota(jnp.int32,(NB,NB),0)<=lax.broadcasted_iota(jnp.int32,(NB,NB),1)
    def fill(k):
        r0=k*NB
        for m in range(nm):
            d=work[m,r0:r0+NB,r0//128*128:r0//128*128+128]
            if r0%128: d=pltpu.roll(d,128-r0%128,axis=1)
            stage[m*NB:(m+1)*NB,:]=jnp.where(lane<NB,d,ident)
    def trail(k):
        r0=k*NB
        end=r0+NB
        lo=end//128*128
        inside=(col>=r0)&(col<end)
        ms=range(nm)
        linv=[stage[m*NB:(m+1)*NB,NB:2*NB] for m in ms]
        rows_m=[jnp.where(inside,(col==idrow+r0).astype(jnp.float32),work[m,r0:end,:]) for m in ms]
        b=[mm_nn(linv[m],rows_m[m]) for m in ms]
        if end<BS:
            up=[jnp.where(upper,stage[m*NB:(m+1)*NB,:NB],0.0) for m in ms]
            left=[rows_m[m][:,lo:]-mm_tn(up[m],b[m][:,lo:]) for m in ms]
            fix=[b[m][:,lo:]+mm_nn(linv[m],left[m]) for m in ms]
            b=[fix[m] if lo==0 else jnp.concatenate([b[m][:,:lo],fix[m]],1) for m in ms]
            cw=colw[:BS-end]
            rest=[mm_tn(b[m][:,lo:],b[m])[end-lo:] for m in ms]
            for m in ms:
                work[m,end:,:]=jnp.where((cw>=r0)&(cw<end),0.0,work[m,end:,:])-rest[m]
        for m in ms:
            work[m,r0:end,:]=b[m]
    def step(kb,c):
        for k in range(BS//NB):
            @pl.when(kb==k)
            def _(k=k):
                fill(k)
        rows=[stage[pl.ds(i,nm,stride=NB),:] for i in range(NB)]
        rows=eliminate(rows,NB)
        for i in range(NB):
            stage[pl.ds(i,nm,stride=NB),:]=rows[i]
        for k in range(BS//NB):
            @pl.when(kb==k)
            def _(k=k):
                trail(k)
        return c
    lax.fori_loop(0,BS//NB,step,0)
    lower=lax.broadcasted_iota(jnp.int32,(BS,BS),0)>=colw
    for s in range(per):
        ql_ref[s]=mm_nt(prods[s],jnp.where(lower,work[s],0.0))
        qr_ref[s]=mm_nt(prods[per+s],jnp.where(lower,work[per+s],0.0))

def soap_call(xor,w,g,first,second,left,right,lb,rb):
    per=w.shape[0]
    sh=jax.ShapeDtypeStruct((per,BS,BS),jnp.float32)
    vm=pl.BlockSpec(memory_space=pltpu.VMEM)
    return pl.pallas_call(functools.partial(soap_kernel,per),
        out_shape=[sh]*7,
        in_specs=[pl.BlockSpec(memory_space=pltpu.SMEM)]+[vm]*8, out_specs=[vm]*7,
        scratch_shapes=[pltpu.VMEM((2*per,BS,BS),jnp.float32),pltpu.VMEM((2*per,BS,BS),jnp.float32),pltpu.VMEM((2*per*NB,128),jnp.float32)],
        compiler_params=pltpu.CompilerParams(vmem_limit_bytes=48*2**20),
        name="soap_update")(xor,w,g,first,second,left,right,lb,rb)


def adam_bias(bias, grad, first, second):
    first_new = BETA_ONE * first + (1.0 - BETA_ONE) * grad
    second_new = BETA_TWO * second + (1.0 - BETA_TWO) * grad * grad
    scaled = (
        first_new
        / (1.0 - BETA_ONE**STEP)
        / (jnp.sqrt(second_new / (1.0 - BETA_TWO**STEP)) + ADAM_EPS)
    )
    return (bias - BIAS_RATE * scaled, first_new, second_new)


def places(index, seq_lens):
    ends = jnp.cumsum(seq_lens)
    segment = jnp.sum((index[:, None] >= ends[None, :]).astype(jnp.int32), 1)
    starts = ends - seq_lens
    picked = segment[:, None] == jnp.arange(seq_lens.shape[0], dtype=jnp.int32)[None, :]
    offset = jnp.sum(jnp.where(picked, starts[None, :], 0), 1)
    return (segment, index - offset)


def swap(x, axis, bit):
    size = lax.axis_size(axis)
    return lax.ppermute(x, axis, [(i, i ^ bit) for i in range(size)])


def gather_xor(x, axis, bits):
    out = x[None]
    for bit in bits:
        out = jnp.concatenate([out, swap(out, axis, bit)], 0)
    return out


def bits_of(size):
    return [1 << i for i in range(size.bit_length() - 1)]


def chip_bits(size):
    return bits_of(size)[1:][::-1] + [1]


def entry_ids(bits):
    ids = [0]
    for bit in bits:
        ids = ids + [i ^ bit for i in ids]
    return ids


def normalize(x, gain, shift):
    centred = x - jnp.mean(x, -1, keepdims=True)
    root = lax.rsqrt(jnp.mean(centred * centred, -1, keepdims=True) + NORM_EPS)
    return centred * root * gain + shift


def layer_kernel(
    chunks, where_ref, emb, cosines, sines, key_meta, query_meta, bias, gain, shift,
    qkv, w_out, w_up, w_down, out, w_qkv, wo, up, down, k_all, v_all, q_own, mix, sems,
):
    group, width = emb.shape
    own = out.shape[0]
    units = w_up.shape[1]
    part = units // chunks
    nbuf = up.shape[0]

    def load_up(j):
        return (
            pltpu.make_async_copy(
                w_up.at[:, j * part : (j + 1) * part], up.at[j % nbuf], sems.at[4 + j % nbuf]
            ),
            pltpu.make_async_copy(
                w_down.at[j * part : (j + 1) * part, :],
                down.at[j % nbuf],
                sems.at[4 + nbuf + j % nbuf],
            ),
        )

    loads = [
        pltpu.make_async_copy(
            qkv.at[:, i * width : (i + 1) * width], w_qkv.at[i], sems.at[i]
        )
        for i in range(3)
    ]
    load_out = pltpu.make_async_copy(w_out, wo, sems.at[3])
    for i in (1, 2, 0):
        loads[i].start()
    load_out.start()
    for j in range(nbuf):
        for copy in load_up(j):
            copy.start()

    lane = lax.broadcasted_iota(jnp.int32, (1, width), 1)
    first_half = lane % HEAD_DIM < ROT // 2

    def rotated(x, cos, sin):
        turned = jnp.where(
            first_half,
            pltpu.roll(x, width - ROT // 2, axis=1),
            pltpu.roll(x, ROT // 2, axis=1),
        )
        reps = width // cos.shape[1]
        return x * jnp.concatenate([cos] * reps, 1) + turned * jnp.concatenate([sin] * reps, 1)

    def attn_in(x):
        return normalize(x.astype(jnp.float32), gain[0:1, :], shift[0:1, :]).astype(jnp.bfloat16)

    loads[1].wait()
    loads[2].wait()
    rows = 256

    def project(i, c):
        at = pl.ds(pl.multiple_of(i * rows, rows), rows)
        x = attn_in(emb[at, :])
        k = jnp.dot(x, w_qkv[1], preferred_element_type=jnp.float32) + bias[:, width : 2 * width]
        k_all[at, :] = rotated(k, cosines[at, :], sines[at, :]).astype(jnp.bfloat16)
        v = jnp.dot(x, w_qkv[2], preferred_element_type=jnp.float32)
        v_all[at, :] = (v + bias[:, 2 * width : 3 * width]).astype(jnp.bfloat16)
        return c

    lax.fori_loop(0, group // rows, project, 0)
    mine = pl.ds(pl.multiple_of(where_ref[0] * own, own), own)
    x_own = emb[mine, :].astype(jnp.float32)
    loads[0].wait()
    q = jnp.dot(attn_in(x_own), w_qkv[0], preferred_element_type=jnp.float32) + bias[:, :width]
    q_own[...] = rotated(q, cosines[mine, :], sines[mine, :]).astype(jnp.bfloat16)

    allowed = (query_meta[:, 0:1] == key_meta[0:1, :]) & (key_meta[1:2, :] <= query_meta[:, 1:2])
    half = lax.broadcasted_iota(jnp.int32, (1, 2 * HEAD_DIM), 1) // HEAD_DIM

    def pair(hp, c):
        at = pl.ds(pl.multiple_of(hp * 2 * HEAD_DIM, 2 * HEAD_DIM), 2 * HEAD_DIM)
        qp, kp, vp = q_own[:, at], k_all[:, at], v_all[:, at]
        outs = []
        for h in range(2):
            qh = jnp.where(half == h, qp, jnp.zeros((), jnp.bfloat16))
            scores = lax.dot_general(
                qh, kp, (((1,), (1,)), ((), ())), preferred_element_type=jnp.float32
            )
            scores = jnp.where(allowed, scores * HEAD_DIM ** (-0.5), MASKED)
            weights = jnp.exp(scores - jnp.max(scores, -1, keepdims=True))
            total = jnp.sum(weights, -1, keepdims=True)
            got = jnp.dot(weights.astype(jnp.bfloat16), vp, preferred_element_type=jnp.float32)
            outs.append(got / total)
        mix[:, at] = jnp.where(half == 0, outs[0], outs[1]).astype(jnp.bfloat16)
        return c

    lax.fori_loop(0, HEADS // 2, pair, 0)
    load_out.wait()
    total = x_own + (
        jnp.dot(mix[...], wo[...], preferred_element_type=jnp.float32)
        + bias[:, 3 * width : 4 * width]
    )
    mlp_in = normalize(x_own, gain[1:2, :], shift[1:2, :]).astype(jnp.bfloat16)
    acc = jnp.zeros((own, width), jnp.float32)
    for j in range(chunks):
        for copy in load_up(j):
            copy.wait()
        lo = 4 * width + j * part
        pre = jnp.dot(mlp_in, up[j % nbuf], preferred_element_type=jnp.float32)
        pre = pre + bias[:, lo : lo + part]
        activ = (0.5 * pre * (1.0 + lax.erf(pre * 0.7071067811865476))).astype(jnp.bfloat16)
        acc = acc + jnp.dot(activ, down[j % nbuf], preferred_element_type=jnp.float32)
        if j + nbuf < chunks:
            for copy in load_up(j + nbuf):
                copy.start()
    total = total + (acc + bias[:, 4 * width + units :])
    out[:, :width] = x_own.astype(jnp.bfloat16)
    out[:, width:] = total.astype(jnp.bfloat16)


def layer_call(where, emb, cosines, sines, key_meta, query_meta, bias, gain, shift, qkv, w_out, w_up, w_down):
    group, width = emb.shape
    own = query_meta.shape[0]
    units = w_up.shape[1]
    chunks = units // width
    nbuf = chunks if group <= 1024 else 2
    vm = pl.BlockSpec(memory_space=pltpu.VMEM)
    hbm = pl.BlockSpec(memory_space=pl.ANY)
    bf = jnp.bfloat16
    return pl.pallas_call(
        functools.partial(layer_kernel, chunks),
        out_shape=jax.ShapeDtypeStruct((own, 2 * width), bf),
        in_specs=[pl.BlockSpec(memory_space=pltpu.SMEM)] + [vm] * 8 + [hbm] * 4,
        out_specs=vm,
        scratch_shapes=[
            pltpu.VMEM((3, width, width), bf),
            pltpu.VMEM((width, width), bf),
            pltpu.VMEM((nbuf, width, units // chunks), bf),
            pltpu.VMEM((nbuf, units // chunks, width), bf),
            pltpu.VMEM((group, width), bf),
            pltpu.VMEM((group, width), bf),
            pltpu.VMEM((own, width), bf),
            pltpu.VMEM((own, width), bf),
            pltpu.SemaphoreType.DMA((4 + 2 * nbuf,)),
        ],
        compiler_params=pltpu.CompilerParams(vmem_limit_bytes=VMEM_LIMIT),
        name="frozen_layer",
    )(where, emb, cosines, sines, key_meta, query_meta, bias, gain, shift, qkv, w_out, w_up, w_down)


def probe_kernel(
    limit, loc_ref, x, slots, bias, gain, shift, table,
    sums, stats, hats, normed, peak, mass, cross,
):
    step = pl.program_id(0)
    steps = pl.num_programs(0)
    count, width = x.shape[0], x.shape[1] // 2
    tile = table.shape[0]
    nblk = width // BS

    @pl.when(step == 0)
    def _():
        def save(i, v):
            centred = v - jnp.mean(v, -1, keepdims=True)
            root = lax.rsqrt(jnp.mean(centred * centred, -1, keepdims=True) + NORM_EPS)
            hat = centred * root
            normed[i * count : (i + 1) * count, :] = (hat * gain[2:3, :] + shift[2:3, :]).astype(
                jnp.bfloat16
            )
            return hat, root

        save(0, x[:, width:].astype(jnp.float32))
        for k in range(2):
            cols = []
            for j in range(nblk):
                total = None
                for i in range(nblk):
                    lo = k * width + i * BS
                    term = jnp.dot(
                        x[:, lo : lo + BS],
                        slots[loc_ref[(k * nblk + i) * nblk + j]],
                        preferred_element_type=jnp.float32,
                    )
                    total = term if total is None else total + term
                cols.append(total)
            v = x[:, k * width : (k + 1) * width].astype(jnp.float32)
            hat, root = save(k + 1, v + jnp.concatenate(cols, 1) + bias[k : k + 1, :])
            hats[k, :, :width] = hat
            hats[k, :, width:] = jnp.broadcast_to(root, (count, 128))
        peak[...] = jnp.full(peak.shape, MASKED, jnp.float32)
        mass[...] = jnp.zeros(mass.shape, jnp.float32)
        cross[...] = jnp.zeros(cross.shape, jnp.float32)
        sums[...] = jnp.zeros(sums.shape, jnp.float32)

    def visit(last):
        w = table[...]
        logits = lax.dot_general(
            normed[...], w, (((1,), (1,)), ((), ())), preferred_element_type=jnp.float32
        )
        if last:
            left = limit - step * tile
            at = lax.broadcasted_iota(jnp.int32, (1, tile), 1)
            logits = jnp.where(at < left, logits, MASKED)
            down = lax.broadcasted_iota(jnp.int32, (tile, 1), 0)
            w = jnp.where(down < left, w, jnp.zeros((), jnp.bfloat16))
        old = peak[...]
        new = jnp.maximum(old, jnp.max(logits, -1, keepdims=True))
        fade = jnp.exp(old - new)
        powers = jnp.exp(logits - new)
        peak[...] = new
        mass[...] = mass[...] * fade + jnp.sum(powers, -1, keepdims=True)
        base, base_fade = powers[:count], fade[:count]
        for k in range(2):
            gap = logits[:count] - logits[(k + 1) * count : (k + 2) * count]
            at = pl.ds(k * count, count)
            cross[at, :] = cross[at, :] * base_fade + jnp.sum(base * gap, -1, keepdims=True)
        sums[...] = sums[...] * fade + jnp.dot(
            powers.astype(jnp.bfloat16), w, preferred_element_type=jnp.float32
        )

    @pl.when(step < steps - 1)
    def _():
        visit(False)

    @pl.when(step == steps - 1)
    def _():
        visit(True)
        at = lax.broadcasted_iota(jnp.int32, (count, 128), 1)
        packed = jnp.zeros((count, 128), jnp.float32)
        for j in range(3):
            packed = jnp.where(at == j, peak[j * count : (j + 1) * count, :], packed)
            packed = jnp.where(at == 3 + j, mass[j * count : (j + 1) * count, :], packed)
        for k in range(2):
            packed = jnp.where(at == 6 + k, cross[k * count : (k + 1) * count, :], packed)
        stats[...] = jnp.transpose(packed)[:8, :]


def probe_call(loc, x, slots, bias, gain, shift, table):
    count, width = x.shape[0], x.shape[1] // 2
    vocab = table.shape[0]
    tile = 640
    steps = -(-vocab // tile)
    f32 = jnp.float32
    vm = pl.BlockSpec(memory_space=pltpu.VMEM)
    return pl.pallas_call(
        functools.partial(probe_kernel, vocab),
        grid=(steps,),
        out_shape=[
            jax.ShapeDtypeStruct((3 * count, width), f32),
            jax.ShapeDtypeStruct((8, count), f32),
            jax.ShapeDtypeStruct((2, count, width + 128), f32),
        ],
        in_specs=[pl.BlockSpec(memory_space=pltpu.SMEM)]
        + [vm] * 5
        + [pl.BlockSpec((tile, width), lambda i: (i, 0))],
        out_specs=[vm, vm, vm],
        scratch_shapes=[
            pltpu.VMEM((3 * count, width), jnp.bfloat16),
            pltpu.VMEM((3 * count, 1), f32),
            pltpu.VMEM((3 * count, 1), f32),
            pltpu.VMEM((2 * count, 1), f32),
        ],
        compiler_params=pltpu.CompilerParams(vmem_limit_bytes=VMEM_LIMIT),
        name="probe_pass",
    )(loc, x, slots, bias, gain, shift, table)


def grad_kernel(dest_ref, x, sums, scale, hats, gain, grads, bias_grad):
    count, width = x.shape[0], x.shape[1] // 2
    nblk = width // BS
    pieces = dest_ref.shape[1]
    rows = BS // pieces
    cols = jnp.transpose(jnp.concatenate([scale[...]] * (128 // scale.shape[0]), 0))
    base = sums[:count, :] * cols[:, 0:1]
    for k in range(2):
        e = (sums[(k + 1) * count : (k + 2) * count, :] * cols[:, k + 1 : k + 2] - base) * gain[2:3, :]
        hat = hats[k, :, :width]
        root = hats[k, :, width : width + 1]
        pulled = e - jnp.mean(e, -1, keepdims=True)
        pulled = (pulled - hat * jnp.mean(e * hat, -1, keepdims=True)) * root
        bias_grad[k : k + 1, :] = jnp.sum(pulled, 0, keepdims=True)
        low = pulled.astype(jnp.bfloat16)
        for i in range(nblk):
            lo = k * width + i * BS
            full = lax.dot_general(
                x[:, lo : lo + BS], low, (((0,), (0,)), ((), ())), preferred_element_type=jnp.float32
            ).astype(jnp.bfloat16)
            for j in range(nblk):
                b = (k * nblk + i) * nblk + j
                for p in range(pieces):
                    grads[dest_ref[b, p]] = full[p * rows : (p + 1) * rows, j * BS : (j + 1) * BS]


def grad_call(dest, x, sums, scale, hats, gain):
    width = x.shape[1] // 2
    pieces = dest.shape[1]
    vm = pl.BlockSpec(memory_space=pltpu.VMEM)
    return pl.pallas_call(
        grad_kernel,
        out_shape=[
            jax.ShapeDtypeStruct((dest.shape[0] * pieces, BS // pieces, BS), jnp.bfloat16),
            jax.ShapeDtypeStruct((2, width), jnp.float32),
        ],
        in_specs=[pl.BlockSpec(memory_space=pltpu.SMEM)] + [vm] * 5,
        out_specs=[vm, vm],
        compiler_params=pltpu.CompilerParams(vmem_limit_bytes=VMEM_LIMIT),
        name="lens_gradient",
    )(dest, x, sums, scale, hats, gain)


def merge(a, b):
    peak = jnp.maximum(a[:3], b[:3])
    fa, fb = jnp.exp(a[:3] - peak), jnp.exp(b[:3] - peak)
    return jnp.concatenate(
        [peak, a[3:6] * fa + b[3:6] * fb, a[6:8] * fa[:1] + b[6:8] * fb[:1]], 0
    )


def halve(x, axis, bit):
    return (x[0].astype(jnp.float32) + swap(x[1], axis, bit).astype(jnp.float32)).astype(x[0].dtype)


def body(
    tokens, loss_position_mask, lengths, owners, embed_in, unembedding_table, frozen_qkv, frozen_out,
    frozen_up, frozen_down, frozen_bias, norm_gain, norm_shift, master_matrix, lens_bias, matrix_first,
    matrix_second, left_stat, right_stat, left_basis, right_basis, bias_first, bias_second,
):
    bf, f32, i32 = jnp.bfloat16, jnp.float32, jnp.int32
    shards, rows = lax.axis_size("vocab"), lax.axis_size("rows")
    where, row = lax.axis_index("vocab"), lax.axis_index("rows")
    group, width = tokens.shape[0], embed_in.shape[1]
    own = group // shards
    nblk = width // BS
    per = master_matrix.shape[0]
    blocks = shards * per
    chips = shards // 2
    vbits, rbits = chip_bits(shards), bits_of(rows)
    entries = np.array(entry_ids(vbits), np.int32)
    entry_at = jnp.array(np.argsort(entries), i32)
    every = jnp.arange(shards, dtype=i32)

    slots = lax.all_gather(master_matrix.astype(bf), "vocab", axis=0, tiled=True)
    biases = gather_xor(lens_bias, "vocab", vbits)
    biases = jnp.take(biases, jnp.take(entry_at, where ^ every), axis=0)
    biases = biases.transpose(1, 0, 2).reshape(2, width)

    def by_class(a):
        return a.reshape(own, shards).T.reshape(-1)

    ids = by_class(tokens)
    index = by_class(jnp.arange(group, dtype=i32))
    mask = by_class(loss_position_mask)
    table_rows = embed_in.shape[0]
    owner = ids // table_rows
    local = ids - where * table_rows
    holds = (owner[:, None] == jnp.arange(shards, dtype=i32)[None, :]).astype(bf)
    before = (jnp.arange(group)[:, None] > jnp.arange(group)[None, :]).astype(bf)
    ahead = jnp.dot(before, holds, preferred_element_type=f32)
    rank = jnp.sum(ahead * holds.astype(f32), 1).astype(i32)
    most = jnp.max(jnp.sum(holds.astype(f32), 0)).astype(i32)
    shared = gather_xor(jnp.concatenate([mask, jnp.full((8,), most, i32)]), "rows", rbits)
    masks = shared[:, :group].reshape(rows, shards, own)
    most = jnp.max(shared[:, group:])

    take = 176 if group <= 1024 else 64
    chip, core = where // 2, where % 2
    apart = (chip - owner // 2) % chips + chips * ((owner % 2) ^ core)
    to_right = [(i, i + 2) for i in range(shards - 2)]
    to_left = [(i + 2, i) for i in range(shards - 2)]

    def fetch(k):
        slot = jnp.arange(take, dtype=i32)[:, None] + k * take
        hit = (owner == where)[None, :] & (rank[None, :] == slot)
        picked = jnp.sum(jnp.where(hit, local[None, :], 0), 1)
        mine = jnp.take(embed_in, picked, axis=0, mode="clip")
        right, left = [mine], [mine]
        for _ in range(1, chips):
            right.append(lax.ppermute(right[-1], "vocab", to_right))
            left.append(lax.ppermute(left[-1], "vocab", to_left))
        near = jnp.concatenate([mine] + [right[o] + left[chips - o] for o in range(1, chips)], 0)
        both = jnp.concatenate([near, swap(near, "vocab", 1)], 0)
        place = rank - k * take
        column = jnp.where((place >= 0) & (place < take), apart * take + place, -1)
        spread = (column[:, None] == jnp.arange(shards * take, dtype=i32)[None, :]).astype(bf)
        return jnp.dot(spread, both, preferred_element_type=f32).astype(bf)

    embedded = fetch(0)
    _, embedded = lax.while_loop(
        lambda c: c[0] * take < most, lambda c: (c[0] + 1, c[1] + fetch(c[0])), (jnp.int32(1), embedded)
    )

    seq_lens = lengths[0]
    segment, position = places(index, seq_lens)
    half = ROT // 2
    lane = jnp.arange(2 * HEAD_DIM) % HEAD_DIM
    freq = 10000.0 ** (-2.0 * (lane % half).astype(f32) / ROT)
    angle = position.astype(f32)[:, None] * freq[None, :]
    turns = (lane < ROT)[None, :]
    cosines = jnp.where(turns, jnp.cos(angle), 1.0)
    sines = jnp.where(turns, jnp.sin(angle) * jnp.where(lane < half, -1.0, 1.0)[None, :], 0.0)
    key_meta = jnp.concatenate([segment[None], index[None], jnp.zeros((6, group), i32)], 0)
    own_seg = lax.dynamic_slice_in_dim(segment, where * own, own)
    own_idx = lax.dynamic_slice_in_dim(index, where * own, own)
    query_meta = jnp.stack([own_seg, own_idx], 1)
    states = layer_call(
        where.reshape(1), embedded, cosines, sines, key_meta, query_meta, frozen_bias.reshape(1, -1),
        norm_gain, norm_shift, frozen_qkv, frozen_out, frozen_up, frozen_down,
    )

    take_rows = max(16, 384 // shards)
    count = take_rows * shards
    mine_masks = lax.dynamic_index_in_dim(masks, where, 1, keepdims=False)
    per_row = jnp.sum(mine_masks, 1)
    lower = (row ^ jnp.arange(rows)) < row
    base = jnp.sum(jnp.where(lower, per_row, 0))
    dealt = base + jnp.cumsum(mine_masks[0]) - mine_masks[0]
    per_class = jnp.sum(masks, (0, 2))
    per_entry = jnp.take(per_class, where ^ entries)
    share = (per_entry - row + rows - 1) // rows
    rounds = -(-jnp.max((per_class + rows - 1) // rows) // take_rows)

    numbers = jnp.arange(blocks, dtype=i32)
    pieces = max(1, rows // per)
    span = per * pieces // rows
    slot_of = jnp.sum(jnp.where(owners[None, :] == numbers[:, None], numbers[None, :], 0), 1)
    device, inner = slot_of // per, slot_of % per
    piece = inner[:, None] * pieces + jnp.arange(pieces, dtype=i32)[None, :]
    part = (piece // span) ^ row
    dest = (jnp.take(entry_at, device ^ where)[:, None] * rows + part) * span + piece % span

    def deal(k):
        target = jnp.arange(rows, dtype=i32) ^ row
        place = jnp.arange(take_rows, dtype=i32) + k * take_rows
        wanted = (place[None, :] * rows + target[:, None]).reshape(-1)
        pick = ((dealt[None, :] == wanted[:, None]) & (mine_masks[0] > 0)[None, :]).astype(bf)
        sent = jnp.dot(pick, states, preferred_element_type=f32).astype(bf)
        sent = sent.reshape(rows, take_rows, 2 * width)
        got = sent[0]
        for e in range(1, rows):
            got = got + swap(sent[e], "rows", e)
        return gather_xor(got, "vocab", vbits).reshape(count, 2 * width)

    def pass_over(k):
        x = deal(k)
        sums, local_stats, hats = probe_call(slot_of, x, slots, biases, norm_gain, norm_shift, unembedding_table)
        stats = local_stats
        for at, bit in enumerate(vbits):
            theirs = swap(stats, "vocab", bit)
            axes = [2] * len(vbits)
            flipped = jnp.flip(theirs.reshape([8] + axes + [take_rows]), len(vbits) - at)
            stats = merge(stats, flipped.reshape(8, count))
        valid = (jnp.arange(take_rows, dtype=i32)[None, :] + k * take_rows < share[:, None]).reshape(-1)
        valid = valid.astype(f32)
        logtot = stats[:3] + jnp.log(stats[3:6])
        diverge = stats[6:8] / stats[3:4] - logtot[:1] + logtot[1:]
        loss = jnp.sum(valid[None, :] * diverge)
        scale = valid[None, :] * jnp.exp(local_stats[:3] - stats[:3]) / stats[3:6]
        scale = jnp.concatenate([scale, jnp.zeros((5, count), f32)], 0)
        grads, bias_grad = grad_call(dest, x, sums, scale, hats, norm_gain)
        return grads, bias_grad, loss

    grads, bias_grad, loss = pass_over(jnp.int32(0))

    def again(c):
        g, b, s = pass_over(c[0])
        return (c[0] + 1, c[1] + g, c[2] + b, c[3] + s)

    _, grads, bias_grad, loss = lax.while_loop(
        lambda c: c[0] < rounds, again, (jnp.int32(1), grads, bias_grad, loss)
    )
    loss_count = jnp.sum(masks).astype(f32)

    small = jnp.concatenate([bias_grad, jnp.full((1, width), jnp.where(where == 0, loss, 0.0))], 0)
    for axis, bits in (("rows", rbits), ("vocab", vbits)):
        for bit in bits:
            small = small + swap(small, axis, bit)
    loss_sum = small[2, 0]
    bias_grad = small[:2]
    bias_cols = lens_bias.shape[1]
    bias_grad = lax.dynamic_slice_in_dim(bias_grad, where * bias_cols, bias_cols, 1)

    g = grads.reshape(2, chips, rows, -1, BS)
    g = halve(g, "vocab", 1)
    cut = [g[..., : BS // 2], g[..., BS // 2 :]]
    for side, bits in enumerate((rbits[::-1], rbits)):
        h = cut[side]
        live = list(range(rows))
        for bit in bits:
            stay = [e for e in live if not e & bit]
            go = [live.index(e | bit) for e in stay]
            keep = [live.index(e) for e in stay]
            h = halve((jnp.stack([h[:, e] for e in keep], 1), jnp.stack([h[:, e] for e in go], 1)), "rows", bit)
            live = stay
        cut[side] = h[:, 0]
    g = jnp.concatenate(cut, -1)
    for bit in vbits[:-1][::-1]:
        n = g.shape[0] // 2
        g = halve((g[:n], g[n:]), "vocab", bit)
    g = g[0]
    full = gather_xor(g, "rows", rbits)
    if per >= rows:
        slot_grad = full.reshape(per, BS, BS)
        turn = row * (per // rows)
    else:
        slot_grad = jnp.take(full, row ^ jnp.arange(rows), axis=0).reshape(per, BS, BS)
        turn = jnp.int32(0)

    (new_matrix, new_first, new_second, new_left, new_right, renewed_left_basis, new_rbasis) = soap_call(
        turn.reshape(1), master_matrix, slot_grad, matrix_first, matrix_second, left_stat, right_stat,
        left_basis, right_basis,
    )
    new_bias, new_bias_first, new_bias_second = adam_bias(lens_bias, bias_grad, bias_first, bias_second)
    return (
        loss_sum, loss_count, new_matrix, new_first, new_second, new_left, new_right, renewed_left_basis,
        new_rbasis, new_bias, new_bias_first, new_bias_second,
    )


def solution(mesh):
    in_specs = (
        P("rows"),
        P("rows"),
        P("rows", None),
        P(),
        P("vocab", None),
        P("vocab", None),
        P(),
        P(),
        P(),
        P(),
        P(),
        P(),
        P(),
        P("vocab", None, None),
        P(None, "vocab"),
        P("vocab", None, None),
        P("vocab", None, None),
        P("vocab", None, None),
        P("vocab", None, None),
        P("vocab", None, None),
        P("vocab", None, None),
        P(None, "vocab"),
        P(None, "vocab"),
    )
    out_specs = (
        P(),
        P(),
        P("vocab", None, None),
        P("vocab", None, None),
        P("vocab", None, None),
        P("vocab", None, None),
        P("vocab", None, None),
        P("vocab", None, None),
        P("vocab", None, None),
        P(None, "vocab"),
        P(None, "vocab"),
        P(None, "vocab"),
    )
    return jax.shard_map(body, mesh=mesh, in_specs=in_specs, out_specs=out_specs, check_vma=False)
```

time: 1520 us -> 410 us (0.27)
  other arithmetic: 632 us -> 26.9 us
  waiting for transfers between devices: 348 us -> 106 us
  local copies, waits for them, and re-layouts: 228 us -> 24.1 us
  matrix products: 180 us -> 7.5 us
  Pallas kernels: 0 us -> 149 us
  blocking collectives: 111 us -> 0 us
  starting transfers between devices: 0.25 us -> 55.9 us
    another operation x31 -> x4, other arithmetic: 451 us -> 0.41 us  [the longest x16 277 us: orthonormal(): factor = jnp.linalg.cholesky(gram)]
    dot_general x24 -> x3, matrix products: 162 us -> 7.5 us  [the longest x1 6.6 us: fetch(): return jnp.dot(spread, both, preferred_element_type=f32).astype(bf)]
    pallas_call x0 -> x4, Pallas kernels: none -> 149 us  [the longest x1 82.1 us: probe_call(): pl.pallas_call(functools.partial(probe_kernel, vocab), grid=(steps,), out...]
    reduce_scatter x2 -> x0, waiting for transfers between devices: 123 us -> none  [the longest x1 87.6 us: body(): lax.psum_scatter(jnp.einsum('yzq,qa->yza', loss_slope, unembedding_table,...]
    psum x1 -> x0, waiting for transfers between devices: 122 us -> none  [body(): slot_grad, bias_grad = lax.psum((slot_grad, bias_grad), ('rows', 'vocab'))]
    ppermute x0 -> x35, waiting for transfers between devices: none -> 106 us  [the longest x29 71.6 us: swap(): return lax.ppermute(x, axis, [(i, i ^ bit) for i in range(size)])]
    reduce_sum x15 -> x8, other arithmetic: 109 us -> 3.39 us  [the longest x1 0.85 us: body(): jnp.sum(jnp.where(owners[None, :] == numbers[:, None], numbers[None, :],...]
    all_gather x3 -> x1, waiting for transfers between devices: 102 us -> 0.01 us  [body(): lax.all_gather(master_matrix.astype(bf), 'vocab', axis=0, tiled=True)]
  transfers between devices with their start and end apart: 6 -> 36, of which waited for: 6 -> 21; matrix products, arithmetic and copies ran while one was open for 4% -> 9% of each run, Pallas kernels for 0% -> 5%
where the time goes in v1:
time: 410 us; the launch traced here: 403 us
  Pallas kernels  149 us (36%)
  waiting for transfers between devices  106 us (26%)
  starting transfers between devices  55.9 us (14%)
  other arithmetic  26.9 us (7%)
  local copies, waits for them, and re-layouts  24.1 us (6%)
  between operations  18.8 us (5%)
  loops' own time  14.7 us (4%)
  matrix products  7.5 us (2%)
    pallas_call x1, Pallas kernels, probe_call(): pl.pallas_call(functools.partial(probe_kernel, vocab), grid=(steps,), out...  82.1 us
    ppermute x29, waiting for transfers between devices, swap(): return lax.ppermute(x, axis, [(i, i ^ bit) for i in range(size)])  71.6 us
    ppermute x29, starting transfers between devices, swap(): return lax.ppermute(x, axis, [(i, i ^ bit) for i in range(size)])  37.3 us
    pallas_call x1, Pallas kernels, soap_call(): pl.pallas_call(functools.partial(soap_kernel, per), out_shape=[sh] * 7, i...  35.4 us
    ppermute x3, waiting for transfers between devices, fetch(): left.append(lax.ppermute(left[-1], 'vocab', to_left))  34.6 us
    pallas_call x1, Pallas kernels, layer_call(): pl.pallas_call(functools.partial(layer_kernel, chunks), out_shape=jax.Sha...  22.2 us
    ppermute x3, starting transfers between devices, fetch(): right.append(lax.ppermute(right[-1], 'vocab', to_right))  14.7 us
    pallas_call x1, Pallas kernels, grad_call(): pl.pallas_call(grad_kernel, out_shape=[jax.ShapeDtypeStruct((dest.shape[0...  9.43 us
  transfers between devices with their start and end apart: 36, of which 21 were waited for; matrix products, arithmetic and copies ran while one was open for 9% of the time, Pallas kernels for 5%

profile of v1, /device:TPU:0, one launch (start us, length us, event | category | flops | bytes accessed | tf_op | source)
XLA Modules:
  0.0 403.2 jit_solution(3031429286698701659)
XLA Ops:
  7.3 0.8 select_reduce_fusion.3.loc_ref
  11.0 7.6 %gather_fusion.2 = bf16[176,1024]{1,0:T(8,128)(2,1)S(1)} fusion(bf16[6288,1024]{1,0:T(8,128)(2,1)} %param.33, s32[1024]{0:T(1024)S(1)} %get-tuple-element.317), kind=kCustom, calls=%fused_computation.2 | custom fusion | bytes 721600 | tf_op jit(solution)/shard_map/jit(_take)/gather | solution.py:593
  18.6 1.3 collective-permute-start.19
  19.9 5.6 %collective-permute-start.18 = (bf16[176,1024]{1,0:T(8,128)(2,1)S(1)}, bf16[176,1024]{1,0:T(8,128)(2,1)S(1)}, u32[]{:S(2)}, u32[]{:S(2)}) collective-permute-start(bf16[176,1024]{1,0:T(8,128)(2,1)S(1)} %gather_fusion.2), channel_id=1, source_target_pairs={{0,2},{1,3},{2,4},{3,5},{4,6},{5,7},{8,10},{9,11},{10,12},{11,13},... | collective-permute-start | bytes 1081352 | tf_op jit(solution)/shard_map/ppermute | solution.py:596
  25.5 3.1 collective-permute-start.31
  30.1 1.5 collective-permute-start.16
  31.6 0.8 convert_element_type.156
  33.8 1.3 collective-permute-start.20
  35.9 4.6 %collective-permute-start.22 = (bf16[176,1024]{1,0:T(8,128)(2,1)S(1)}, bf16[176,1024]{1,0:T(8,128)(2,1)S(1)}, u32[]{:S(2)}, u32[]{:S(2)}) collective-permute-start(bf16[176,1024]{1,0:T(8,128)(2,1)S(1)} %collective-permute-done.18), channel_id=1, source_target_pairs={{0,2},{1,3},{2,4},{3,5},{4,6},{5,7},{8,10},{9,11},{10,12},{11,13},... | collective-permute-start | bytes 1081352 | tf_op jit(solution)/shard_map/ppermute | solution.py:596
  40.5 18.4 %collective-permute-done.20 = bf16[176,1024]{1,0:T(8,128)(2,1)S(1)} collective-permute-done((bf16[176,1024]{1,0:T(8,128)(2,1)S(1)}, bf16[176,1024]{1,0:T(8,128)(2,1)S(1)}, u32[]{:S(2)}, u32[]{:S(2)}) %collective-permute-start.20) | collective-permute-done | bytes 360480 | tf_op jit(solution)/shard_map/ppermute | solution.py:597
  58.9 1.3 collective-permute-start.21
  60.2 1.7 collective-permute-start.17
  64.0 4.6 %collective-permute-start.23 = (bf16[176,1024]{1,0:T(8,128)(2,1)S(1)}, bf16[176,1024]{1,0:T(8,128)(2,1)S(1)}, u32[]{:S(2)}, u32[]{:S(2)}) collective-permute-start(bf16[176,1024]{1,0:T(8,128)(2,1)S(1)} %collective-permute-done.22), channel_id=1, source_target_pairs={{0,2},{1,3},{2,4},{3,5},{4,6},{5,7},{8,10},{9,11},{10,12},{11,13},... | collective-permute-start | bytes 1081352 | tf_op jit(solution)/shard_map/ppermute | solution.py:596
  68.5 16.2 %collective-permute-done.21 = bf16[176,1024]{1,0:T(8,128)(2,1)S(1)} collective-permute-done((bf16[176,1024]{1,0:T(8,128)(2,1)S(1)}, bf16[176,1024]{1,0:T(8,128)(2,1)S(1)}, u32[]{:S(2)}, u32[]{:S(2)}) %collective-permute-start.21) | collective-permute-done | bytes 360480 | tf_op jit(solution)/shard_map/ppermute | solution.py:597
  84.8 0.8 constant_dynamic-update-slice_fusion.8
  85.6 0.8 constant_dynamic-update-slice_fusion.7
  86.5 0.9 constant_dynamic-update-slice_fusion.6
  90.9 3.1 fusion.22
  94.0 2.6 constant_dynamic-update-slice_fusion.5
  96.5 6.6 %fusion.16 = bf16[1024,1024]{1,0:T(8,128)(2,1)} fusion(bf16[1408,1024]{1,0:T(8,128)(2,1)} %constant_dynamic-update-slice_fusion.5, s32[1024]{0:T(1024)S(1)} %get-tuple-element.274), kind=kOutput, calls=%fused_computation.75 | convolution fusion | flops 2955280384 | bytes 4984832 | tf_op jit(solution)/shard_map/dot_general | solution.py:603
  103.1 7.1 %while.24 = (s32[]{:T(128)}, bf16[1024,1024]{1,0:T(8,128)(2,1)}, s32[]{:T(128)}, s32[1024]{0:T(1024)S(1)}, s32[1024]{0:T(1024)S(1)}, /*index=5*/s32[]{:T(128)}, ...) while((s32[]{:T(128)}, bf16[1024,1024]{1,0:T(8,128)(2,1)}, ...), condition=%wide.region_11.12_spmd, body=%wide.region_9.11_spmd.sunk | while | flops 2964988928 | bytes 61380540 | solution.py:606
  110.3 22.2 %frozen_layer.1 = bf16[128,2048]{1,0:T(8,128)(2,1)S(1)} custom-call(s32[1]{0:T(128)} %bitcast.13.where_ref, bf16[1024,1024]{1,0:T(8,128)(2,1)} %get-tuple-element.167.emb, f32[1024,128]{1,0:T(8,128)} %get-tuple-element.312.cosines, f32[1024,128]{1,0:T(8,128)} %get-tuple-element.311.sines, s32[8,1024]{1,0:T(8,128)} %add_add_fusion.key_meta, ...), custom_call_target="tpu_custom_call" | custom-call | tf_op jit(solution)/shard_map/frozen_layer/pallas_call | solution.py:348
  133.0 3.0 collective-permute-start.27
  136.5 4.2 %collective-permute-done.25 = bf16[48,2048]{1,0:T(8,128)(2,1)S(1)} collective-permute-done((bf16[48,2048]{1,0:T(8,128)(2,1)S(1)}, bf16[48,2048]{1,0:T(8,128)(2,1)S(1)}, u32[]{:S(2)}, u32[]{:S(2)}) %collective-permute-start.25) | collective-permute-done | bytes 196640 | tf_op jit(solution)/shard_map/ppermute | solution.py:193
  140.7 4.9 %collective-permute-done.27 = bf16[48,2048]{1,0:T(8,128)(2,1)S(1)} collective-permute-done((bf16[48,2048]{1,0:T(8,128)(2,1)S(1)}, bf16[48,2048]{1,0:T(8,128)(2,1)S(1)}, u32[]{:S(2)}, u32[]{:S(2)}) %collective-permute-start.27) | collective-permute-done | bytes 196640 | tf_op jit(solution)/shard_map/ppermute | solution.py:193
  145.6 1.4 collective-permute-done.26
  147.0 3.9 collective-permute-start.28
  150.9 8.3 %collective-permute-done.28 = bf16[1,48,2048]{2,1,0:T(8,128)(2,1)S(1)} collective-permute-done((bf16[1,48,2048]{2,1,0:T(8,128)(2,1)S(1)}, bf16[1,48,2048]{2,1,0:T(8,128)(2,1)S(1)}, u32[]{:S(2)}, u32[]{:S(2)}) %collective-permute-start.28) | collective-permute-done | bytes 196640 | tf_op jit(solution)/shard_map/ppermute | solution.py:193
  160.7 1.5 collective-permute-start.32
  162.2 7.4 %collective-permute-done.29 = bf16[2,48,2048]{2,1,0:T(8,128)(2,1)S(1)} collective-permute-done((bf16[2,48,2048]{2,1,0:T(8,128)(2,1)S(1)}, bf16[2,48,2048]{2,1,0:T(8,128)(2,1)S(1)}, u32[]{:S(2)}, u32[]{:S(2)}) %collective-permute-start.29) | collective-permute-done | bytes 393248 | tf_op jit(solution)/shard_map/ppermute | solution.py:193
  169.6 1.0 pad_maximum_fusion.8
  171.1 1.6 collective-permute-done.33
  174.2 2.5 pad_maximum_fusion.6
  176.6 82.1 %probe_pass.2 = (f32[1152,1024]{1,0:T(8,128)}, f32[8,384]{1,0:T(8,128)}, f32[2,384,1152]{2,1,0:T(8,128)}) custom-call(s32[32]{0:T(128)S(1)} %select_reduce_fusion.3.loc_ref, bf16[384,2048]{1,0:T(8,128)(2,1)} %bitcast.93, bf16[32,256,256]{2,1,0:T(8,128)(2,1)} %all-gather.2.cloned.1.call-done.slots, f32[2,1024]{1,0:T(2,128)S(1)} %select_bitcast_fusion.bias, ...), custom_call_target="tpu_custom_call" | custom-call | tf_op jit(solution)/shard_map/probe_pass/pallas_call | solution.py:463
  258.7 3.1 collective-permute-start.34
  261.9 1.9 collective-permute-done.34
  264.4 0.8 multiply_add_fusion.7
  266.0 1.8 collective-permute-start.35
  267.9 1.9 collective-permute-done.35
  273.9 9.4 %lens_gradient.2 = (bf16[32,256,256]{2,1,0:T(8,128)(2,1)}, f32[2,1024]{1,0:T(2,128)S(1)}) custom-call(s32[32,1]{1,0:T(8,128)S(1)} %fusion.37.dest_ref, bf16[384,2048]{1,0:T(8,128)(2,1)} %bitcast.94, f32[1152,1024]{1,0:T(8,128)} %get-tuple-element.168.sums, f32[8,384]{1,0:T(8,128)} %concatenate.105.scale, f32[2,384,1152]{2,1,0:T(8,128)} %get-tuple-element.170.hats, ...), custom_call_target="tpu_custom_call" | custom-call | tf_op jit(solution)/shard_map/lens_gradient/pallas_call | solution.py:516
  284.0 7.6 %while.25 = (s32[]{:T(128)}, bf16[32,256,256]{2,1,0:T(8,128)(2,1)}, f32[2,1024]{1,0:T(2,128)S(1)}, f32[]{:T(128)}, s32[]{:T(128)}, /*index=5*/s32[128]{0:T(128)S...) while((s32[]{:T(128)}, bf16[32,256,256]{2,1,0:T(8,128)(2,1)}, ...), condition=%wide.region_21.22_spmd, body=%wide.region_19.21_spmd.sunk | while | flops 106891688 | bytes 80534776 | solution.py:686
  291.6 2.7 fusion.71
  295.0 3.8 collective-permute-done.42
  300.3 1.5 collective-permute-start.45
  301.9 11.9 %collective-permute-done.43 = bf16[4,2,256,128]{3,2,0,1:T(8,128)(2,1)S(1)} collective-permute-done((bf16[4,2,256,128]{3,2,0,1:T(8,128)(2,1)S(1)}, bf16[4,2,256,128]{3,2,0,1:T(8,128)(2,1)S(1)}, u32[]{:S(2)}, u32[]{:S(2)}) %collective-permute-start.43) | collective-permute-done | bytes 524320 | tf_op jit(solution)/shard_map/ppermute | solution.py:193
  314.0 1.5 collective-permute-start.44
  316.3 5.6 %collective-permute-done.44 = bf16[4,1,256,128]{3,2,0,1:T(8,128)(2,1)S(1)} collective-permute-done((bf16[4,1,256,128]{3,2,0,1:T(8,128)(2,1)S(1)}, bf16[4,1,256,128]{3,2,0,1:T(8,128)(2,1)S(1)}, u32[]{:S(2)}, u32[]{:S(2)}) %collective-permute-start.44) | collective-permute-done | bytes 262176 | tf_op jit(solution)/shard_map/ppermute | solution.py:193
  321.9 1.4 collective-permute-done.46
  323.3 1.8 collective-permute-start.47
  325.2 4.8 %collective-permute-done.47 = bf16[2,256,256]{2,1,0:T(8,128)(2,1)S(1)} collective-permute-done((bf16[2,256,256]{2,1,0:T(8,128)(2,1)S(1)}, bf16[2,256,256]{2,1,0:T(8,128)(2,1)S(1)}, u32[]{:S(2)}, u32[]{:S(2)}) %collective-permute-start.47) | collective-permute-done | bytes 262176 | tf_op jit(solution)/shard_map/ppermute | solution.py:193
  330.1 3.0 collective-permute-start.48
  334.4 3.1 collective-permute-done.48
  337.5 0.9 add_convert_fusion.5
  339.1 1.2 collective-permute-start.38
  340.4 3.1 collective-permute-done.49
  344.7 1.7 collective-permute-start.39
  346.4 3.0 collective-permute-done.39
  349.4 1.5 collective-permute-start.40
  350.9 2.3 collective-permute-done.40
  354.9 1.3 multiply_subtract_fusion
  356.2 1.0 pad_maximum_fusion.10.g_ref
  357.2 1.2 copy-done.3
  358.4 1.2 copy-done.4
  359.7 35.4 %soap_update.1 = (f32[4,256,256]{2,1,0:T(8,128)}, f32[4,256,256]{2,1,0:T(8,128)}, f32[4,256,256]{2,1,0:T(8,128)}, f32[4,256,256]{2,1,0:T(8,128)}, f32[4,256,256]...) custom-call(s32[1]{0:T(128)} %bitcast.37.where_ref, f32[4,256,256]{2,1,0:T(8,128)S(1)} %copy-done, ...), custom_call_target="tpu_custom_call" | custom-call | tf_op jit(solution)/shard_map/soap_update/pallas_call | solution.py:163
  (207 shorter events, 28.5 us)
Async XLA Ops:
  7.2 18.3 %copy-start.15 = (f32[2,128]{1,0:T(2,128)S(1)}, f32[2,128]{1,0:T(2,128)}, u32[]{:S(2)}) copy-start(f32[2,128]{1,0:T(2,128)} %param.43) | copy-start | bytes 3076
  7.2 22.7 %copy-start.16 = (s32[1024]{0:T(1024)S(1)}, s32[1024]{0:T(1024)}, u32[]{:S(2)}) copy-start(s32[1024]{0:T(1024)} %param.30) | copy-start | bytes 12292
  7.2 24.4 %copy-start = (f32[4,256,256]{2,1,0:T(8,128)S(1)}, f32[4,256,256]{2,1,0:T(8,128)}, u32[]{:S(2)}) copy-start(f32[4,256,256]{2,1,0:T(8,128)} %w_ref.1) | copy-start | bytes 3145732
  7.2 169.4 %all-gather.2.cloned.1.call-start = ((), (), s32[]{:S(2)}) async-start(), calls=%async_computation | async-start | bytes 4718592 | tf_op jit(solution)/shard_map/all_gather | solution.py:560
  10.6 22.0 %copy-start.18 = (s32[1,5]{1,0:T(1,128)S(1)}, s32[1,5]{1,0:T(1,128)}, u32[]{:S(2)}) copy-start(s32[1,5]{1,0:T(1,128)} %param.31) | copy-start | bytes 64
  11.0 51.6 %copy-start.5 = (s32[8]{0:T(128)S(1)}, s32[8]{0:T(128)}, u32[]{:S(2)}) copy-start(s32[8]{0:T(128)} %constant.301.clone) | copy-start | bytes 100
  18.6 15.2 %collective-permute-start.19 = (bf16[176,1024]{1,0:T(8,128)(2,1)S(1)}, bf16[176,1024]{1,0:T(8,128)(2,1)S(1)}, u32[]{:S(2)}, u32[]{:S(2)}) collective-permute-start(bf16[176,1024]{1,0:T(8,128)(2,1)S(1)} %gather_fusion.2), channel_id=1, source_target_pairs={{2,0},{3,1},{4,2},{5,3},{6,4},{7,5},{10,8},{11,9},{12,10},{13,11},... | collective-permute-start | bytes 1081352 | tf_op jit(solution)/shard_map/ppermute | solution.py:597
  19.9 16.0 %collective-permute-start.18 = (bf16[176,1024]{1,0:T(8,128)(2,1)S(1)}, bf16[176,1024]{1,0:T(8,128)(2,1)S(1)}, u32[]{:S(2)}, u32[]{:S(2)}) collective-permute-start(bf16[176,1024]{1,0:T(8,128)(2,1)S(1)} %gather_fusion.2), channel_id=1, source_target_pairs={{0,2},{1,3},{2,4},{3,5},{4,6},{5,7},{8,10},{9,11},{10,12},{11,13},... | collective-permute-start | bytes 1081352 | tf_op jit(solution)/shard_map/ppermute | solution.py:596
  25.5 135.3 %collective-permute-start.31 = (f32[1,2,128]{2,1,0:T(2,128)S(1)}, f32[1,2,128]{2,1,0:T(2,128)S(1)}, u32[]{:S(2)}, u32[]{:S(2)}) collective-permute-start(f32[1,2,128]{2,1,0:T(2,128)S(1)} %bitcast.111), channel_id=1, source_target_pairs={{0,4},{1,5},{2,6},{3,7},{4,0},{5,1},{6,2},{7,3},{8,12},{9,13},{10,... | collective-permute-start | bytes 3080 | tf_op jit(solution)/shard_map/ppermute | solution.py:193
  30.1 30.1 %collective-permute-start.16 = (s32[1,1032]{1,0:T(1,128)S(1)}, s32[1,1032]{1,0:T(1,128)S(1)}, u32[]{:S(2)}, u32[]{:S(2)}) collective-permute-start(s32[1,1032]{1,0:T(1,128)S(1)} %broadcast_in_dim.186), channel_id=1, source_target_pairs={{0,8},{8,0},{16,24},{24,16},{1,9},{9,1},{17,25},{25,17},{2,10},{10... | collective-permute-start | bytes 12392 | tf_op jit(solution)/shard_map/ppermute | solution.py:193
  33.8 25.1 %collective-permute-start.20 = (bf16[176,1024]{1,0:T(8,128)(2,1)S(1)}, bf16[176,1024]{1,0:T(8,128)(2,1)S(1)}, u32[]{:S(2)}, u32[]{:S(2)}) collective-permute-start(bf16[176,1024]{1,0:T(8,128)(2,1)S(1)} %collective-permute-done.19), channel_id=1, source_target_pairs={{2,0},{3,1},{4,2},{5,3},{6,4},{7,5},{10,8},{11,9},{12,10},{13,11},... | collective-permute-start | bytes 1081352 | tf_op jit(solution)/shard_map/ppermute | solution.py:597
  35.9 28.0 %collective-permute-start.22 = (bf16[176,1024]{1,0:T(8,128)(2,1)S(1)}, bf16[176,1024]{1,0:T(8,128)(2,1)S(1)}, u32[]{:S(2)}, u32[]{:S(2)}) collective-permute-start(bf16[176,1024]{1,0:T(8,128)(2,1)S(1)} %collective-permute-done.18), channel_id=1, source_target_pairs={{0,2},{1,3},{2,4},{3,5},{4,6},{5,7},{8,10},{9,11},{10,12},{11,13},... | collective-permute-start | bytes 1081352 | tf_op jit(solution)/shard_map/ppermute | solution.py:596
  58.9 25.9 %collective-permute-start.21 = (bf16[176,1024]{1,0:T(8,128)(2,1)S(1)}, bf16[176,1024]{1,0:T(8,128)(2,1)S(1)}, u32[]{:S(2)}, u32[]{:S(2)}) collective-permute-start(bf16[176,1024]{1,0:T(8,128)(2,1)S(1)} %collective-permute-done.20), channel_id=1, source_target_pairs={{2,0},{3,1},{4,2},{5,3},{6,4},{7,5},{10,8},{11,9},{12,10},{13,11},... | collective-permute-start | bytes 1081352 | tf_op jit(solution)/shard_map/ppermute | solution.py:597
  60.2 3.7 collective-permute-start.17
  64.0 22.5 %collective-permute-start.23 = (bf16[176,1024]{1,0:T(8,128)(2,1)S(1)}, bf16[176,1024]{1,0:T(8,128)(2,1)S(1)}, u32[]{:S(2)}, u32[]{:S(2)}) collective-permute-start(bf16[176,1024]{1,0:T(8,128)(2,1)S(1)} %collective-permute-done.22), channel_id=1, source_target_pairs={{0,2},{1,3},{2,4},{3,5},{4,6},{5,7},{8,10},{9,11},{10,12},{11,13},... | collective-permute-start | bytes 1081352 | tf_op jit(solution)/shard_map/ppermute | solution.py:596
  87.5 6.5 %collective-permute-start.24 = (bf16[704,1024]{1,0:T(8,128)(2,1)S(1)}, bf16[704,1024]{1,0:T(8,128)(2,1)}, u32[]{:S(2)}, u32[]{:S(2)}) collective-permute-start(bf16[704,1024]{1,0:T(8,128)(2,1)S(1)} %pad_maximum_fusion.7), channel_id=1, source_target_pairs={{0,1},{1,0},{2,3},{3,2},{4,5},{5,4},{6,7},{7,6},{8,9},{9,8},{10,11... | collective-permute-start | bytes 4325384 | tf_op jit(solution)/shard_map/ppermute | solution.py:193
  103.1 7.1 %copy-start.9 = (f32[3,1024]{1,0:T(4,128)S(1)}, f32[3,1024]{1,0:T(4,128)}, u32[]{:S(2)}) copy-start(f32[3,1024]{1,0:T(4,128)} %gain.5) | copy-start | bytes 36868
  103.1 7.1 %copy-start.13 = (f32[3,1024]{1,0:T(4,128)S(1)}, f32[3,1024]{1,0:T(4,128)}, u32[]{:S(2)}) copy-start(f32[3,1024]{1,0:T(4,128)} %shift.3) | copy-start | bytes 36868
  132.9 7.8 %collective-permute-start.25 = (bf16[48,2048]{1,0:T(8,128)(2,1)S(1)}, bf16[48,2048]{1,0:T(8,128)(2,1)S(1)}, u32[]{:S(2)}, u32[]{:S(2)}) collective-permute-start(bf16[48,2048]{1,0:T(8,128)(2,1)S(1)} %get-tuple-element.301), channel_id=1, source_target_pairs={{0,8},{8,0},{16,24},{24,16},{1,9},{9,1},{17,25},{25,17},{2,10},{10... | collective-permute-start | bytes 589832 | tf_op jit(solution)/shard_map/ppermute | solution.py:193
  133.0 12.6 %collective-permute-start.27 = (bf16[48,2048]{1,0:T(8,128)(2,1)S(1)}, bf16[48,2048]{1,0:T(8,128)(2,1)S(1)}, u32[]{:S(2)}, u32[]{:S(2)}) collective-permute-start(bf16[48,2048]{1,0:T(8,128)(2,1)S(1)} %get-tuple-element.302), channel_id=1, source_target_pairs={{0,24},{8,16},{16,8},{24,0},{1,25},{9,17},{17,9},{25,1},{2,26},{10... | collective-permute-start | bytes 589832 | tf_op jit(solution)/shard_map/ppermute | solution.py:193
  136.0 11.0 %collective-permute-start.26 = (bf16[48,2048]{1,0:T(8,128)(2,1)S(1)}, bf16[48,2048]{1,0:T(8,128)(2,1)S(1)}, u32[]{:S(2)}, u32[]{:S(2)}) collective-permute-start(bf16[48,2048]{1,0:T(8,128)(2,1)S(1)} %get-tuple-element.303), channel_id=1, source_target_pairs={{0,16},{8,24},{16,0},{24,8},{1,17},{9,25},{17,1},{25,9},{2,18},{10... | collective-permute-start | bytes 589832 | tf_op jit(solution)/shard_map/ppermute | solution.py:193
  147.0 12.3 %collective-permute-start.28 = (bf16[1,48,2048]{2,1,0:T(8,128)(2,1)S(1)}, bf16[1,48,2048]{2,1,0:T(8,128)(2,1)S(1)}, u32[]{:S(2)}, u32[]{:S(2)}) collective-permute-start(bf16[1,48,2048]{2,1,0:T(8,128)(2,1)S(1)} %fusion.28), channel_id=1, source_target_pairs={{0,4},{1,5},{2,6},{3,7},{4,0},{5,1},{6,2},{7,3},{8,12},{9,13},{10,... | collective-permute-start | bytes 589832 | tf_op jit(solution)/shard_map/ppermute | solution.py:193
  159.3 10.2 %collective-permute-start.29 = (bf16[2,48,2048]{2,1,0:T(8,128)(2,1)S(1)}, bf16[2,48,2048]{2,1,0:T(8,128)(2,1)S(1)}, u32[]{:S(2)}, u32[]{:S(2)}) collective-permute-start(bf16[2,48,2048]{2,1,0:T(8,128)(2,1)S(1)} %pad_maximum_fusion.11), channel_id=1, source_target_pairs={{0,2},{1,3},{2,0},{3,1},{4,6},{5,7},{6,4},{7,5},{8,10},{9,11},{10,... | collective-permute-start | bytes 1179656 | tf_op jit(solution)/shard_map/ppermute | solution.py:193
  160.7 9.8 %collective-permute-start.32 = (f32[2,2,128]{2,1,0:T(2,128)S(1)}, f32[2,2,128]{2,1,0:T(2,128)S(1)}, u32[]{:S(2)}, u32[]{:S(2)}) collective-permute-start(f32[2,2,128]{2,1,0:T(2,128)S(1)} %pad_maximum_fusion.18), channel_id=1, source_target_pairs={{0,2},{1,3},{2,0},{3,1},{4,6},{5,7},{6,4},{7,5},{8,10},{9,11},{10,... | collective-permute-start | bytes 6152 | tf_op jit(solution)/shard_map/ppermute | solution.py:193
  170.5 3.6 collective-permute-start.30
  170.6 2.2 collective-permute-start.33
  258.7 5.0 %collective-permute-start.34 = (f32[8,384]{1,0:T(8,128)}, f32[8,384]{1,0:T(8,128)S(1)}, u32[]{:S(2)}, u32[]{:S(2)}) collective-permute-start(f32[8,384]{1,0:T(8,128)} %get-tuple-element.169), channel_id=1, source_target_pairs={{0,4},{1,5},{2,6},{3,7},{4,0},{5,1},{6,2},{7,3},{8,12},{9,13},{10,... | collective-permute-start | bytes 36872 | tf_op jit(solution)/shard_map/ppermute | solution.py:193
  266.0 3.8 collective-permute-start.35
  270.4 1.5 collective-permute-start.36
  294.4 4.3 %collective-permute-start.42 = (bf16[4,4,256,256]{3,2,0,1:T(8,128)(2,1)S(1)}, bf16[4,4,256,256]{3,2,0,1:T(8,128)(2,1)S(1)}, u32[]{:S(2)}, u32[]{:S(2)}) collective-permute-start(bf16[4,4,256,256]{3,2,0,1:T(8,128)(2,1)S(1)} %copy.83), channel_id=1, source_target_pairs={{0,1},{1,0},{2,3},{3,2},{4,5},{5,4},{6,7},{7,6},{8,9},{9,8},{10,11... | collective-permute-start | bytes 6291464 | tf_op jit(solution)/shard_map/ppermute | solution.py:193
  299.5 14.3 %collective-permute-start.43 = (bf16[4,2,256,128]{3,2,0,1:T(8,128)(2,1)S(1)}, bf16[4,2,256,128]{3,2,0,1:T(8,128)(2,1)S(1)}, u32[]{:S(2)}, u32[]{:S(2)}) collective-permute-start(bf16[4,2,256,128]{3,2,0,1:T(8,128)(2,1)S(1)} %stack.29), channel_id=1, source_target_pairs={{0,16},{8,24},{16,0},{24,8},{1,17},{9,25},{17,1},{25,9},{2,18},{10... | collective-permute-start | bytes 1572872 | tf_op jit(solution)/shard_map/ppermute | solution.py:193
  300.3 15.1 %collective-permute-start.45 = (bf16[4,2,256,128]{3,2,0,1:T(8,128)(2,1)S(1)}, bf16[4,2,256,128]{3,2,0,1:T(8,128)(2,1)S(1)}, u32[]{:S(2)}, u32[]{:S(2)}) collective-permute-start(bf16[4,2,256,128]{3,2,0,1:T(8,128)(2,1)S(1)} %pad_maximum_fusion.9), channel_id=1, source_target_pairs={{0,8},{8,0},{16,24},{24,16},{1,9},{9,1},{17,25},{25,17},{2,10},{10... | collective-permute-start | bytes 1572872 | tf_op jit(solution)/shard_map/ppermute | solution.py:193
  314.0 7.8 %collective-permute-start.44 = (bf16[4,1,256,128]{3,2,0,1:T(8,128)(2,1)S(1)}, bf16[4,1,256,128]{3,2,0,1:T(8,128)(2,1)S(1)}, u32[]{:S(2)}, u32[]{:S(2)}) collective-permute-start(bf16[4,1,256,128]{3,2,0,1:T(8,128)(2,1)S(1)} %slice.541), channel_id=1, source_target_pairs={{0,8},{8,0},{16,24},{24,16},{1,9},{9,1},{17,25},{25,17},{2,10},{10... | collective-permute-start | bytes 786440 | tf_op jit(solution)/shard_map/ppermute | solution.py:193
  315.6 39.3 %copy-start.17 = (f32[2,128]{1,0:T(2,128)S(1)}, f32[2,128]{1,0:T(2,128)}, u32[]{:S(2)}) copy-start(f32[2,128]{1,0:T(2,128)} %param.50) | copy-start | bytes 3076
  315.7 41.5 %copy-start.1 = (f32[4,256,256]{2,1,0:T(8,128)S(1)}, f32[4,256,256]{2,1,0:T(8,128)}, u32[]{:S(2)}) copy-start(f32[4,256,256]{2,1,0:T(8,128)} %first_ref.1) | copy-start | bytes 3145732
  315.7 41.5 %copy-start.2 = (f32[4,256,256]{2,1,0:T(8,128)S(1)}, f32[4,256,256]{2,1,0:T(8,128)}, u32[]{:S(2)}) copy-start(f32[4,256,256]{2,1,0:T(8,128)} %second_ref.1) | copy-start | bytes 3145732
  315.7 7.6 %collective-permute-start.46 = (bf16[4,1,256,128]{3,2,0,1:T(8,128)(2,1)S(1)}, bf16[4,1,256,128]{3,2,0,1:T(8,128)(2,1)S(1)}, u32[]{:S(2)}, u32[]{:S(2)}) collective-permute-start(bf16[4,1,256,128]{3,2,0,1:T(8,128)(2,1)S(1)} %slice.547), channel_id=1, source_target_pairs={{0,16},{8,24},{16,0},{24,8},{1,17},{9,25},{17,1},{25,9},{2,18},{10... | collective-permute-start | bytes 786440 | tf_op jit(solution)/shard_map/ppermute | solution.py:193
  323.3 6.6 %collective-permute-start.47 = (bf16[2,256,256]{2,1,0:T(8,128)(2,1)S(1)}, bf16[2,256,256]{2,1,0:T(8,128)(2,1)S(1)}, u32[]{:S(2)}, u32[]{:S(2)}) collective-permute-start(bf16[2,256,256]{2,1,0:T(8,128)(2,1)S(1)} %pad_maximum_fusion.12), channel_id=1, source_target_pairs={{0,2},{1,3},{2,0},{3,1},{4,6},{5,7},{6,4},{7,5},{8,10},{9,11},{10,... | collective-permute-start | bytes 786440 | tf_op jit(solution)/shard_map/ppermute | solution.py:193
  330.1 7.4 %collective-permute-start.48 = (bf16[1,256,256]{2,1,0:T(8,128)(2,1)S(1)}, bf16[1,256,256]{2,1,0:T(8,128)(2,1)}, u32[]{:S(2)}, u32[]{:S(2)}) collective-permute-start(bf16[1,256,256]{2,1,0:T(8,128)(2,1)S(1)} %slice.551), channel_id=1, source_target_pairs={{0,4},{1,5},{2,6},{3,7},{4,0},{5,1},{6,2},{7,3},{8,12},{9,13},{10,... | collective-permute-start | bytes 393224 | tf_op jit(solution)/shard_map/ppermute | solution.py:193
  333.7 5.4 %collective-permute-start.37 = (f32[3,1024]{1,0:T(4,128)S(1)}, f32[3,1024]{1,0:T(4,128)S(1)}, u32[]{:S(2)}, u32[]{:S(2)}) collective-permute-start(f32[3,1024]{1,0:T(4,128)S(1)} %concatenate.106), channel_id=1, source_target_pairs={{0,8},{8,0},{16,24},{24,16},{1,9},{9,1},{17,25},{25,17},{2,10},{10... | collective-permute-start | bytes 36872 | tf_op jit(solution)/shard_map/ppermute | solution.py:193
  338.5 5.0 %collective-permute-start.49 = (bf16[1,256,256]{2,1,0:T(8,128)(2,1)S(1)}, bf16[1,256,256]{2,1,0:T(8,128)(2,1)S(1)}, u32[]{:S(2)}, u32[]{:S(2)}) collective-permute-start(bf16[1,256,256]{2,1,0:T(8,128)(2,1)S(1)} %add_convert_fusion.5), channel_id=1, source_target_pairs={{0,8},{8,0},{16,24},{24,16},{1,9},{9,1},{17,25},{25,17},{2,10},{10... | collective-permute-start | bytes 393224 | tf_op jit(solution)/shard_map/ppermute | solution.py:193
  339.1 5.6 %collective-permute-start.38 = (f32[3,1024]{1,0:T(4,128)S(1)}, f32[3,1024]{1,0:T(4,128)S(1)}, u32[]{:S(2)}, u32[]{:S(2)}) collective-permute-start(f32[3,1024]{1,0:T(4,128)S(1)} %pad_add_fusion.2), channel_id=1, source_target_pairs={{0,16},{8,24},{16,0},{24,8},{1,17},{9,25},{17,1},{25,9},{2,18},{10... | collective-permute-start | bytes 36872 | tf_op jit(solution)/shard_map/ppermute | solution.py:193
  344.2 12.0 %collective-permute-start.50 = (bf16[2,256,256]{2,1,0:T(8,128)(2,1)}, bf16[2,256,256]{2,1,0:T(8,128)(2,1)}, u32[]{:S(2)}, u32[]{:S(2)}) collective-permute-start(bf16[2,256,256]{2,1,0:T(8,128)(2,1)} %pad_maximum_fusion.13), channel_id=1, source_target_pairs={{0,16},{8,24},{16,0},{24,8},{1,17},{9,25},{17,1},{25,9},{2,18},{10... | collective-permute-start | bytes 786440 | tf_op jit(solution)/shard_map/ppermute | solution.py:193
  344.7 4.7 %collective-permute-start.39 = (f32[3,1024]{1,0:T(4,128)S(1)}, f32[3,1024]{1,0:T(4,128)S(1)}, u32[]{:S(2)}, u32[]{:S(2)}) collective-permute-start(f32[3,1024]{1,0:T(4,128)S(1)} %add.520), channel_id=1, source_target_pairs={{0,4},{1,5},{2,6},{3,7},{4,0},{5,1},{6,2},{7,3},{8,12},{9,13},{10,... | collective-permute-start | bytes 36872 | tf_op jit(solution)/shard_map/ppermute | solution.py:193
  349.4 3.7 collective-permute-start.40
  353.2 1.2 collective-permute-start.41
  357.2 1.2 copy-start.3
  358.4 1.2 copy-start.4
Sparse Core Ops, SparseCore 0:
  32.6 55.6 all-gather.1
